TPU v7x, 256 devices: a whole 4x4x8 slice. The times are simulated.
256 devices in a mesh: member: 2 (over y_lo), lat: 8 (over z), lon: 16 (over y_hi, x, core).
Axes of the slice: x: 4, y: 4 (y_hi: 2, y_lo: 2; y = y_hi * 2 + y_lo), z: 8, core: 2. Of those that a mesh axis runs over, the one named last changes fastest.
Arguments:
- fields: bfloat16 [2, 2, 48, 192, 768], P('member', None, 'lat', 'lon'), may hold values from -6 to 6
- cotangent: bfloat16 [2, 2, 48, 192, 768], P('member', None, 'lat', 'lon'), may hold values from -6 to 6
- qkv_weight: bfloat16 [2, 768, 2304], replicated, may hold values from -0.21875 to 0.21875
- out_weight: bfloat16 [2, 768, 768], replicated, may hold values from -0.21875 to 0.21875
- norm_gain: float32 [2, 768], replicated, may hold values from 0.25 to 1.75
- bias_table: float32 [2, 8, 759, 24], P(None, 'lat'), may hold values from -4 to 253
- bias_index: int32 [144, 144], replicated, may hold values from 0 to 758
- region: int32 [2, 48, 192], P(None, 'lat', 'lon'), may hold values from 0 to 1
Outputs:
- output: bfloat16 [2, 2, 48, 192, 768], P('member', None, 'lat', 'lon')
- grad_fields: bfloat16 [2, 2, 48, 192, 768], P('member', None, 'lat', 'lon')
- grad_out: float32 [2, 768, 768], P(None, 'lat', 'lon')
All inputs are finite; a program needn't handle non-finite values.
Results may differ from a plain program's by a relative error of at most 0.03.
Values may be sent and summed in bfloat16 or wider, within the bound.
No kernel may reach another device: no remote copies, remote signals or barrier semaphores. Data moves between devices by JAX's collectives and lax.ppermute only.
A program may use at most 128 MiB of HBM per device.

v0:
```python
import functools

import jax
import jax.numpy as jnp
import numpy as np
from jax import lax
from jax.experimental import pallas as pl
from jax.experimental.pallas import tpu as pltpu
from jax.sharding import PartitionSpec as P

LEVELS = 2
WIN_LAT = 6
WIN_LON = 12
HALF_LAT = WIN_LAT // 2
HALF_LON = WIN_LON // 2
WIN = LEVELS * WIN_LAT * WIN_LON
QUAD = WIN // 4
D = 768
HEADS = 24
HEAD_DIM = D // HEADS
GROUP = 128 // HEAD_DIM
GROUPS = HEADS // GROUP
NREL = 759
CHUNKS = 6
DEPTH = 24
TAIL = WIN - 128
SCALE = HEAD_DIM ** (-0.5)
EPS = 1e-05

bf16 = jnp.bfloat16
f32 = jnp.float32


def quad_order():
    token = np.arange(WIN)
    quad, inside = token // QUAD, token % QUAD
    level = inside // (HALF_LAT * HALF_LON)
    row = inside // HALF_LON % HALF_LAT + HALF_LAT * (quad // 2)
    col = inside % HALF_LON + HALF_LON * (quad % 2)
    stored = (row * WIN_LON + col) * LEVELS + level
    window = (level * WIN_LAT + row) * WIN_LON + col
    return row * LEVELS + level, col, stored, window


def constants():
    line, col, stored, window = quad_order()
    order = np.eye(WIN, dtype=np.float32)[stored]
    window_order = np.eye(WIN, dtype=np.float32)[window]
    at_line = np.eye(LEVELS * WIN_LAT, dtype=np.float32)[line]
    at_col = np.eye(WIN_LON, dtype=np.float32)[col]
    return order, window_order, at_line, at_col


def contract(left, right, dims):
    return lax.dot_general(left, right, ((dims[:1], dims[1:]), ((), ())), preferred_element_type=f32)


def mm(left, right):
    return contract(left, right, (1, 0))


def mm_t(left, right):
    return contract(left, right, (1, 1))


def eye(size):
    rows = lax.broadcasted_iota(jnp.int32, (size, size), 0)
    cols = lax.broadcasted_iota(jnp.int32, (size, size), 1)
    return (rows == cols).astype(f32).astype(bf16)


def head_masks():
    lane = lax.broadcasted_iota(jnp.int32, (1, 128), 1)
    masks = []
    for head in range(GROUP):
        inside = jnp.logical_and(lane >= head * HEAD_DIM, lane < (head + 1) * HEAD_DIM)
        masks.append(inside.astype(f32).astype(bf16))
    return masks


def layer_norm(values_f):
    centred = values_f - jnp.mean(values_f, axis=-1, keepdims=True)
    variance = jnp.mean(centred * centred, axis=-1, keepdims=True)
    inv_std = lax.rsqrt(variance + EPS)
    return centred * inv_std, inv_std


def place_index(index_ref, order, wide_ref):
    index_f = index_ref[...].astype(f32)
    high = jnp.floor(index_f * 0.125)
    low = index_f - high * 8.0
    parts = []
    for part in (high, low):
        half = mm(order, part.astype(bf16)).astype(bf16)
        parts.append(mm_t(half, order))
    moved = parts[0] * 8.0 + parts[1]
    wide_ref[:, :WIN] = (moved + 0.5).astype(jnp.int32)
    wide_ref[:, WIN:] = jnp.zeros((WIN, 256 - WIN), jnp.int32)
    lane = lax.broadcasted_iota(jnp.int32, (DEPTH, 128), 1)
    packed = jnp.zeros((DEPTH, 128), jnp.int32)
    for strip in range(WIN // DEPTH):
        piece = wide_ref[strip * DEPTH : (strip + 1) * DEPTH, 128:256]
        if strip:
            piece = pltpu.roll(piece, strip * TAIL, axis=1)
        inside = jnp.logical_and(lane >= strip * TAIL, lane < (strip + 1) * TAIL)
        packed = jnp.where(inside, piece, packed)
    wide_ref[:DEPTH, 128:256] = packed


def lane_gather(row, index):
    numbers = lax.GatherDimensionNumbers(
        offset_dims=(),
        collapsed_slice_dims=(1,),
        start_index_map=(1,),
        operand_batching_dims=(0,),
        start_indices_batching_dims=(0,),
    )
    mode = lax.GatherScatterMode.PROMISE_IN_BOUNDS
    return lax.gather(row, index[..., None], numbers, slice_sizes=(1, 1), mode=mode)


def gather_bias(wide_ref, table_ref, bias_ref, rows_ref, tail_ref, mask_ref, done=None):
    for head in range(HEADS):
        rows_ref[head, :, :NREL] = jnp.broadcast_to(table_ref[head : head + 1, :], (8, NREL))

    def look_up(index, store):
        low_part = jnp.bitwise_and(index, 127)
        high_part = jnp.right_shift(index, 7)
        for head in range(HEADS):
            found = jnp.zeros((8, 128), f32)
            for chunk in range(CHUNKS):
                row = rows_ref[head, :, chunk * 128 : (chunk + 1) * 128]
                found = jnp.where(high_part == chunk, lane_gather(row, low_part), found)
            store(head, found)

    def main_strip(strip, carry):
        lines = pl.ds(pl.multiple_of(strip * 8, 8), 8)
        mask = None if mask_ref is None else mask_ref[lines, :128]

        def store(head, found):
            bias_ref[head, lines, :128] = found if mask is None else found + mask

        look_up(wide_ref[lines, :128], store)
        return carry

    def tail_strip(strip, carry):
        lines = pl.ds(pl.multiple_of(strip * 8, 8), 8)

        def store(head, found):
            tail_ref[head, lines, :] = found

        look_up(wide_ref[lines, 128:256], store)
        return carry

    def unpack(head, carry):
        rest = tail_ref[head]
        for strip in range(WIN // DEPTH):
            lines = slice(strip * DEPTH, (strip + 1) * DEPTH)
            piece = rest if strip == 0 else pltpu.roll(rest, 128 - strip * TAIL, axis=1)
            piece = piece[:, :TAIL]
            if mask_ref is not None:
                piece = piece + mask_ref[lines, 128:WIN]
            bias_ref[head, lines, 128:WIN] = piece
        return carry

    lax.fori_loop(0, DEPTH // 8, tail_strip, 0, unroll=3)
    lax.fori_loop(0, HEADS, unpack, 0, unroll=4)
    for third in range(3):
        lax.fori_loop(third * 6, third * 6 + 6, main_strip, 0, unroll=6)
        if done is not None:
            done(third)


def project_qkv(hidden, w_parts, qkv_ref):
    for part in range(3):
        qkv_ref[:, part * D : (part + 1) * D] = mm(hidden, w_parts(part)[...]).astype(bf16)


def stack_heads(values, masks):
    return jnp.concatenate([values * mask for mask in masks], axis=0)


def merge_heads(stacked):
    lane = lax.broadcasted_iota(jnp.int32, (1, 128), 1)
    merged = stacked[:WIN]
    for head in range(1, GROUP):
        later = lane >= head * HEAD_DIM
        merged = jnp.where(later, stacked[head * WIN : (head + 1) * WIN], merged)
    return merged


def group_cols(group, part):
    return slice(part * D + group * 128, part * D + (group + 1) * 128)


def attend(qkv_ref, bias_ref, probs_ref, mixed_ref):
    masks = head_masks()
    ones = jnp.ones((WIN, 128), bf16)
    for group in range(GROUPS):
        heads = slice(group * GROUP, (group + 1) * GROUP)
        query = qkv_ref[:, group_cols(group, 0)]
        key = qkv_ref[:, group_cols(group, 1)]
        value = qkv_ref[:, group_cols(group, 2)]
        scores = mm_t(stack_heads(query, masks), key) * SCALE
        scores = scores + bias_ref[heads].reshape(GROUP * WIN, WIN)
        exponent = jnp.exp(scores - jnp.max(scores, axis=-1, keepdims=True)).astype(bf16)
        product = mm(exponent, jnp.concatenate([value, ones], axis=1))
        share = 1.0 / product[:, 128:]
        weights = exponent.astype(f32) * jnp.concatenate([share, share[:, : WIN - 128]], axis=1)
        probs_ref[heads] = weights.astype(bf16).reshape(GROUP, WIN, WIN)
        mixed = merge_heads(product[:, :128] * share)
        mixed_ref[:, group_cols(group, 0)] = mixed.astype(bf16)


def back_attend(grad, qkv_ref, probs_ref, mixed_ref, w_out_ref, grad_mixed_ref, turned_ref, rows_ref):
    masks = head_masks()
    unit = eye(256)
    small = eye(WIN)
    minus = -jnp.ones((WIN, 128), bf16)
    grad_mixed_ref[...] = mm_t(grad, w_out_ref[...]).astype(bf16)
    for part in range(3):
        cols = slice(part * 256, (part + 1) * 256)
        turned_ref[0, cols, :] = mm_t(unit, grad_mixed_ref[:, cols]).astype(bf16)
        turned_ref[1, cols, :] = mm_t(unit, qkv_ref[:, cols]).astype(bf16)
    for group in range(GROUPS):
        heads = slice(group * GROUP, (group + 1) * GROUP)
        cols = group_cols(group, 0)
        grad_mixed = grad_mixed_ref[:, cols]
        key = qkv_ref[:, group_cols(group, 1)]
        value = qkv_ref[:, group_cols(group, 2)]
        weights = probs_ref[heads].reshape(GROUP * WIN, WIN)
        probs = weights.astype(f32)
        left = stack_heads(grad_mixed, masks)
        if mixed_ref is None:
            grad_weights = mm_t(left, value)
            moved = grad_weights - jnp.sum(grad_weights * probs, axis=-1, keepdims=True)
        else:
            inner = grad_mixed.astype(f32) * mixed_ref[:, cols].astype(f32)
            left = jnp.concatenate([left, stack_heads(inner.astype(bf16), masks)], axis=1)
            moved = mm_t(left, jnp.concatenate([value, minus], axis=1))
        grad_scores = (probs * moved * SCALE).astype(bf16)
        rows_ref[:, cols] = merge_heads(mm(grad_scores, key)).astype(bf16)
        for inner in range(GROUP):
            head = group * GROUP + inner
            lines = slice(head * HEAD_DIM, (head + 1) * HEAD_DIM)
            tokens = slice(inner * WIN, (inner + 1) * WIN)
            turned_ref[2, lines, :] = mm(turned_ref[1, lines, :], grad_scores[tokens]).astype(bf16)
            turned_ref[3, lines, :] = mm(turned_ref[0, lines, :], weights[tokens]).astype(bf16)
    for part in range(3):
        cols = slice(part * 256, (part + 1) * 256)
        for which in (1, 2):
            out = slice(which * D + part * 256, which * D + (part + 1) * 256)
            rows_ref[:, out] = mm_t(small, turned_ref[1 + which, cols, :]).astype(bf16)


def back_norm(grad_f, normed, inv_std, gain, rows_ref, w_parts):
    grad_hidden = jnp.zeros((WIN, D), f32)
    for part in range(3):
        grad_hidden += mm_t(rows_ref[:, part * D : (part + 1) * D], w_parts(part)[...])
    grad_normed = grad_hidden * gain
    mean_one = jnp.mean(grad_normed, axis=-1, keepdims=True)
    mean_two = jnp.mean(grad_normed * normed, axis=-1, keepdims=True)
    return grad_f + inv_std * (grad_normed - mean_one - normed * mean_two)


def put_quads(values_f, hold_ref, quad_refs, section):
    hold_ref[...] = values_f
    cols = slice(section * D, (section + 1) * D)
    for quad in range(4):
        quad_refs[quad][:, cols] = hold_ref[quad * QUAD : (quad + 1) * QUAD, :].astype(bf16)


def take_quads(quad_refs, hold_ref, section):
    cols = slice(section * D, (section + 1) * D)
    for quad in range(4):
        hold_ref[quad * QUAD : (quad + 1) * QUAD, :] = quad_refs[quad][:, cols].astype(f32)
    return hold_ref[...]


def first_forward(
    blocks, bias_ref, rows_ref, tail_ref, hold_ref, mixed_ref,
):
    quads = blocks.outs[:4]
    wide_ref, input_ref, qkv_ref, probs_ref = blocks.outs[4:]
    place_index(blocks.get(1), blocks.get(0)[...], wide_ref)
    blocks.put(4)
    order = blocks.get(4)[...]
    values_f = mm(order, blocks.get(3)[...].reshape(WIN, D))
    input_ref[...] = values_f.astype(bf16)
    blocks.put(5)
    normed, _ = layer_norm(values_f)
    hidden = (normed * blocks.get(5)[0:1, :]).astype(bf16)

    def project(third):
        cols = slice(third * D, (third + 1) * D)
        qkv_ref[:, cols] = mm(hidden, blocks.get(6 + third)[...]).astype(bf16)

    gather_bias(wide_ref, blocks.get(2), bias_ref, rows_ref, tail_ref, None, project)
    blocks.put(6)
    attend(qkv_ref, bias_ref, probs_ref, mixed_ref)
    blocks.put(7)
    put_quads(mm(order, blocks.get(10)[...].reshape(WIN, D)), hold_ref, quads, 1)
    mixed = mixed_ref[...]
    put_quads(mixed.astype(f32), hold_ref, quads, 2)
    result = input_ref[...].astype(f32) + mm(mixed, blocks.get(9)[...])
    put_quads(result, hold_ref, quads, 0)
    for quad in range(4):
        blocks.put(quad)


def second_bias(blocks, rows_ref, tail_ref, mask_ref, sems):
    region_ref, edge_ref, bias_ref = blocks.get(0), blocks.get(1), blocks.outs[0]
    labels = jnp.concatenate([region_ref[row] for row in range(WIN_LAT)], axis=0)
    labels = labels.astype(f32) * 2.0 - 1.0
    at_line, at_col = blocks.get(2)[...], blocks.get(3)[...]
    column = jnp.sum(mm(at_line, labels.astype(bf16)) * at_col.astype(f32), axis=1, keepdims=True)
    signs = jnp.broadcast_to(column, (WIN, 128)).astype(bf16)
    same = mm_t(signs, signs) > 0.0
    half = WIN // 2
    rows = lax.broadcasted_iota(jnp.int32, (WIN, WIN), 0) >= half
    cols = lax.broadcasted_iota(jnp.int32, (WIN, WIN), 1) >= half
    across = jnp.logical_and(jnp.logical_xor(rows, cols), edge_ref[0] != 0)
    allowed = jnp.logical_and(same, jnp.logical_not(across))
    mask_ref[...] = jnp.where(allowed, 0.0, -jnp.inf)

    def done(third):
        rows = pl.ds(third * (WIN // 3), WIN // 3)
        blocks.put(0, (slice(None), rows), sems.at[third])

    gather_bias(blocks.get(5), blocks.get(4), bias_ref, rows_ref, tail_ref, mask_ref, done)


def pick_columns(core, width):
    rows = lax.broadcasted_iota(jnp.int32, (D // 2, D), 0)
    cols = lax.broadcasted_iota(jnp.int32, (D // 2, D), 1)
    part = jnp.floor((rows.astype(f32) + 0.5) * (1.0 / width)).astype(jnp.int32)
    return (cols == rows + width * (part + core)).astype(f32).astype(bf16)


def second_block(
    width, blocks, hold_ref, mixed_ref, qkv_ref, probs_ref, grad_mixed_ref, turned_ref, grad_rows_ref
):
    leaving = blocks.outs[:4]
    own_ref, other_ref = blocks.outs[4:]
    arrived = [blocks.get(quad) for quad in range(4)]
    values_f = take_quads(arrived, hold_ref, 0)
    normed, inv_std = layer_norm(values_f)
    gain = blocks.get(4)[1:2, :]
    hidden = (normed * gain).astype(bf16)

    def w_parts(part):
        return blocks.get(5 + part)

    project_qkv(hidden, w_parts, qkv_ref)
    attend(qkv_ref, blocks.get(8), probs_ref, mixed_ref)
    w_out_ref = blocks.get(9)
    result = values_f + mm(mixed_ref[...], w_out_ref[...])
    put_quads(result, hold_ref, leaving, 1)
    grad_f = take_quads(arrived, hold_ref, 1)
    grad = grad_f.astype(bf16)
    first_mixed = take_quads(arrived, hold_ref, 2).astype(bf16)
    half = D // 2
    core = blocks.get(10)[0]
    own, other = pick_columns(core, width), pick_columns(1 - core, width)
    for ref, pick in ((own_ref, own), (other_ref, other)):
        ref[:, :D] = first_mixed
        ref[:, D : 2 * D] = mixed_ref[...]
        ref[:, 2 * D + half :] = mm_t(grad, pick).astype(bf16)
    back_attend(
        grad, qkv_ref, probs_ref, mixed_ref, w_out_ref, grad_mixed_ref, turned_ref, grad_rows_ref
    )
    grad_input = back_norm(grad_f, normed, inv_std, gain, grad_rows_ref, w_parts)
    first_grad = grad_input.astype(bf16)
    other_ref[:, 2 * D : 2 * D + half] = mm_t(first_grad, other).astype(bf16)
    blocks.put(5)
    put_quads(grad_input, hold_ref, leaving, 0)
    for quad in range(4):
        blocks.put(quad)
    own_ref[:, 2 * D : 2 * D + half] = mm_t(first_grad, own).astype(bf16)
    blocks.put(4)


def weight_terms(blocks, sems):
    terms_ref = blocks.outs[0]
    n_parts, rows, _ = terms_ref.shape
    n_parts //= 2
    half = n_parts * rows
    unit = eye(half)
    packs = (blocks.get(0), blocks.get(1))
    for block in range(2):
        cols = slice(2 * D + block * half, 2 * D + (block + 1) * half)
        total = jnp.zeros((half, D), f32)
        for pack in packs:
            turned = mm_t(unit, pack[:, cols]).astype(bf16)
            total += mm(turned, pack[:, block * D : (block + 1) * D])
        for part in range(n_parts):
            piece = total[part * rows : (part + 1) * rows, :].astype(bf16)
            terms_ref[block * n_parts + part] = piece
        blocks.put(0, pl.ds(block * n_parts, n_parts), sems.at[block])


def sum_plane(blocks):
    parts_ref, out_ref = blocks.get(0), blocks.outs[0]
    total = parts_ref[0].astype(f32)
    for part in range(1, parts_ref.shape[0]):
        total += parts_ref[part].astype(f32)
    copies = 2
    places = out_ref.shape[0] // copies
    width = D // places
    for place in range(places):
        piece = total[:, place * width : (place + 1) * width].astype(bf16)
        for copy in range(copies):
            out_ref[copy * places + place, :, :width] = piece
    blocks.put(0)


def sum_lat(scale, blocks):
    parts_ref, out_ref = blocks.get(0), blocks.outs[0]
    width = out_ref.shape[2]
    count = parts_ref.shape[0] // 2
    for block in range(2):
        total = parts_ref[block * count].astype(f32)
        for part in range(1, count):
            total += parts_ref[block * count + part].astype(f32)
        out_ref[block] = total[:, :width] * scale
    blocks.put(0)


def first_backward(blocks, hold_ref, grad_mixed_ref, turned_ref, grad_rows_ref):
    grad_fields_ref, output_ref = blocks.outs
    normed, inv_std = layer_norm(blocks.get(4)[...].astype(f32))
    arrived = [blocks.get(quad) for quad in range(4)]
    grad_f = take_quads(arrived, hold_ref, 0)
    qkv_ref, probs_ref, w_out_ref = blocks.get(5), blocks.get(6), blocks.get(7)
    back_attend(
        grad_f.astype(bf16), qkv_ref, probs_ref, None, w_out_ref, grad_mixed_ref, turned_ref,
        grad_rows_ref,
    )
    gain = blocks.get(8)[0:1, :]
    grad_input = back_norm(
        grad_f, normed, inv_std, gain, grad_rows_ref, lambda part: blocks.get(10 + part)
    )
    back_order = blocks.get(9)[...]
    shape = grad_fields_ref.shape
    grad_input = mm(back_order, grad_input.astype(bf16))
    grad_fields_ref[...] = grad_input.astype(bf16).reshape(shape)
    blocks.put(0)
    result = mm(back_order, take_quads(arrived, hold_ref, 1).astype(bf16))
    output_ref[...] = result.astype(bf16).reshape(shape)
    blocks.put(1)


class Blocks:
    def __init__(self, in_refs, in_holds, out_refs, out_holds, in_sems, out_sems):
        self.ins, self.outs, self.waiting, self.leaving = [], [], {}, []
        self.out_refs, self.out_sems = out_refs, out_sems
        for place, (ref, hold) in enumerate(zip(in_refs, in_holds)):
            if hold is not None:
                copy = pltpu.make_async_copy(ref, hold, in_sems.at[place])
                copy.start()
                self.waiting[place] = copy
            self.ins.append(ref if hold is None else hold)
        for ref, hold in zip(out_refs, out_holds):
            self.outs.append(ref if hold is None else hold)

    def get(self, place):
        if place in self.waiting:
            self.waiting.pop(place).wait()
        return self.ins[place]

    def put(self, place, part=None, sem=None):
        source, target = self.outs[place], self.out_refs[place]
        if part is not None:
            source, target = source.at[part], target.at[part]
        sem = self.out_sems.at[place] if sem is None else sem
        copy = pltpu.make_async_copy(source, target, sem)
        copy.start()
        self.leaving.append(copy)


HBM, SMEM = pltpu.HBM, pltpu.SMEM


def call(kernel, ins, outs, scratch, flops, name, mib=63):
    holds = []
    for array, space, index in ins:
        if space is HBM:
            shape = array.shape
            if index is not None:
                shape = array.shape[1:] if isinstance(index, int) else index[0]
            holds.append(pltpu.VMEM(shape, array.dtype))
    for shape, kind, space in outs:
        if space is HBM:
            holds.append(pltpu.VMEM(shape, kind))
    n_in, n_out = len(ins), len(outs)

    def run(*refs):
        in_refs = []
        for ref, (_, _, index) in zip(refs, ins):
            if index is not None:
                ref = ref.at[index] if isinstance(index, int) else index[1](ref)
            in_refs.append(ref)
        out_refs = refs[n_in : n_in + n_out]
        spare = list(refs[n_in + n_out : n_in + n_out + len(holds)])
        in_sems, out_sems, *rest = refs[n_in + n_out + len(holds) :]
        in_holds = [spare.pop(0) if space is HBM else None for _, space, _ in ins]
        out_holds = [spare.pop(0) if space is HBM else None for _, _, space in outs]
        blocks = Blocks(in_refs, in_holds, out_refs, out_holds, in_sems, out_sems)
        kernel(blocks, *rest)
        for copy in blocks.leaving:
            copy.wait()

    return pl.pallas_call(
        run,
        out_shape=[jax.ShapeDtypeStruct(shape, kind) for shape, kind, _ in outs],
        in_specs=[pl.BlockSpec(memory_space=space) for _, space, _ in ins],
        out_specs=[pl.BlockSpec(memory_space=space) for _, _, space in outs],
        scratch_shapes=holds
        + [pltpu.SemaphoreType.DMA((n_in,)), pltpu.SemaphoreType.DMA((n_out,))]
        + scratch,
        compiler_params=pltpu.CompilerParams(vmem_limit_bytes=mib * 1024 * 1024),
        cost_estimate=pl.CostEstimate(flops=flops, bytes_accessed=4_000_000, transcendentals=0),
        name=name,
    )(*[array for array, _, _ in ins])


def exchange(quads, forward):
    n_lat, n_pair, n_core = (lax.axis_size(axis) for axis in ("lat", "pair", "core"))
    n_lon = n_pair * n_core
    by = -1 if forward else 1

    def moved(shard, over_lat, over_lon):
        pairs = []
        for row in range(n_lat):
            for col in range(n_lon):
                to = (row + by * over_lat) % n_lat * n_lon + (col + by * over_lon) % n_lon
                pairs.append((row * n_lon + col, to))
        return lax.ppermute(shard, ("lat", "pair", "core"), pairs)

    if forward:
        return (
            quads[3],
            moved(quads[2], 0, 1),
            moved(quads[1], 1, 0),
            moved(quads[0], 1, 1),
        )
    return (
        moved(quads[3], 1, 1),
        moved(quads[2], 1, 0),
        moved(quads[1], 0, 1),
        quads[0],
    )


def reduce_terms(own, other, returned, after, scale):
    n_lat, n_member = lax.axis_size("lat"), lax.axis_size("member")
    n_pair, n_core = lax.axis_size("pair"), lax.axis_size("core")
    rows = D // (n_pair * n_core)
    width = D // n_lat
    partner = lax.ppermute(other, "core", [(i, (i + 1) % n_core) for i in range(n_core)])
    (terms,) = call(
        weight_terms,
        [(own, HBM, None), (partner, HBM, None)],
        [((n_member * n_pair, rows, D), bf16, HBM)],
        [pltpu.SemaphoreType.DMA((2,))],
        3_000_000_000,
        "weight_terms",
        16,
    )
    terms, *_ = lax.optimization_barrier((terms, *returned))
    parts = lax.all_to_all(terms, ("member", "pair"), 0, 0, tiled=True)
    (plane_sum,) = call(
        sum_plane,
        [(parts, HBM, None), (after, pl.ANY, None)],
        [((n_member * n_lat, rows, -(-width // 128) * 128), bf16, HBM)],
        [],
        5_000_000,
        "sum_plane",
        16,
    )
    parts = lax.all_to_all(plane_sum, ("member", "lat"), 0, 0, tiled=True)
    (total,) = call(
        functools.partial(sum_lat, scale),
        [(parts, HBM, None)],
        [((2, rows, width), f32, HBM)],
        [],
        1_000_000,
        "sum_lat",
        8,
    )
    return total.transpose(0, 2, 1)


def body(fields, cotangent, qkv_weight, out_weight, norm_gain, bias_table, bias_index, region):
    order, window_order, at_line, at_col = constants()
    window_order = jnp.asarray(window_order, bf16)
    back_order = jnp.asarray(order.T, bf16)
    order = jnp.asarray(order, bf16)
    at_line, at_col = jnp.asarray(at_line, bf16), jnp.asarray(at_col, bf16)
    edge = (lax.axis_index("lat") == lax.axis_size("lat") - 1).astype(jnp.int32).reshape(1)
    n_pair, n_core = lax.axis_size("pair"), lax.axis_size("core")
    core = lax.axis_index("core")

    def qkv_parts(block):
        def part_of(part):
            return (D, D), lambda ref: ref.at[block, :, pl.ds(part * D, D)]

        return [(qkv_weight, HBM, part_of(part)) for part in range(3)]

    gather_scratch = [pltpu.VMEM((HEADS, 8, CHUNKS * 128), f32), pltpu.VMEM((HEADS, DEPTH, 128), f32)]
    hold = pltpu.VMEM((WIN, D), f32)
    mixed_scratch = pltpu.VMEM((WIN, D), bf16)
    back_scratch = [
        pltpu.VMEM((WIN, D), bf16),
        pltpu.VMEM((4, D, WIN), bf16),
        pltpu.VMEM((WIN, 3 * D), bf16),
    ]
    cells = (WIN_LAT * WIN_LON, LEVELS, D)
    table = bias_table.transpose(0, 1, 3, 2).reshape(2, HEADS, NREL)
    first = call(
        first_forward,
        [
            (window_order, HBM, None),
            (bias_index, HBM, None),
            (table, HBM, 0),
            (fields.transpose(0, 2, 3, 1, 4).reshape(cells), HBM, None),
            (order, HBM, None),
            (norm_gain, HBM, None),
            *qkv_parts(0),
            (out_weight, HBM, 0),
            (cotangent.transpose(0, 2, 3, 1, 4).reshape(cells), HBM, None),
        ],
        [((QUAD, 3 * D), bf16, HBM)] * 4
        + [
            ((WIN, 256), jnp.int32, HBM),
            ((WIN, D), bf16, HBM),
            ((WIN, 3 * D), bf16, HBM),
            ((HEADS, WIN, WIN), bf16, HBM),
        ],
        [pltpu.VMEM((HEADS, WIN, WIN), f32)] + gather_scratch + [hold, mixed_scratch],
        1_000_000_000,
        "first_forward",
    )
    wide, inputs, qkv_one, probs_one = first[4:]
    shifted = exchange(first[:4], True)
    (bias_two,) = call(
        second_bias,
        [
            (region.transpose(1, 0, 2), HBM, None),
            (edge, SMEM, None),
            (at_line, HBM, None),
            (at_col, HBM, None),
            (table, HBM, 1),
            (wide, HBM, None),
        ],
        [((HEADS, WIN, WIN), f32, HBM)],
        gather_scratch + [pltpu.VMEM((WIN, WIN), f32), pltpu.SemaphoreType.DMA((3,))],
        5_000_000_000,
        "second_bias",
    )
    second = call(
        functools.partial(second_block, D // (n_pair * n_core)),
        [(quad, HBM, None) for quad in shifted]
        + [
            (norm_gain, HBM, None),
            *qkv_parts(1),
            (bias_two, HBM, None),
            (out_weight, HBM, 1),
            (core.astype(jnp.int32).reshape(1), SMEM, None),
        ],
        [((QUAD, 2 * D), bf16, HBM)] * 4 + [((WIN, 3 * D), bf16, HBM)] * 2,
        [hold, mixed_scratch, pltpu.VMEM((WIN, 3 * D), bf16), pltpu.VMEM((HEADS, WIN, WIN), bf16)]
        + back_scratch,
        15_000_000_000,
        "second_block",
    )
    returned = exchange(second[:4], False)
    grad_fields, output = call(
        first_backward,
        [(quad, HBM, None) for quad in returned]
        + [
            (inputs, HBM, None),
            (qkv_one, HBM, None),
            (probs_one, HBM, None),
            (out_weight, HBM, 0),
            (norm_gain, HBM, None),
            (back_order, HBM, None),
        ]
        + qkv_parts(0),
        [(cells, bf16, HBM)] * 2,
        [hold] + back_scratch,
        9_000_000_000,
        "first_backward",
        61,
    )

    token_total = lax.axis_size("member") * lax.axis_size("lat") * n_pair * n_core * WIN
    scale = float(token_total) ** (-0.5)
    grad_out = reduce_terms(second[4], second[5], returned, grad_fields, scale)

    def whole(values):
        grid = values.reshape(1, WIN_LAT, WIN_LON, LEVELS, D)
        return grid.transpose(0, 3, 1, 2, 4)

    return whole(output), whole(grad_fields), grad_out


def solution(mesh):
    n_member, n_lat, n_lon = mesh.devices.shape
    split = mesh.devices.reshape(n_member, n_lat, n_lon // 2, 2)
    mesh = jax.sharding.Mesh(split, ("member", "lat", "pair", "core"))
    lon = ("pair", "core")
    grid = P("member", None, "lat", lon, None)
    placed = (grid, grid, P(), P(), P(), P(None, "lat", None, None), P(), P(None, "lat", lon))
    return jax.shard_map(
        body,
        mesh=mesh,
        in_specs=placed,
        out_specs=(grid, grid, P(None, "lat", lon)),
        check_vma=False,
    )
```

profile of v0, /device:TPU:32, one launch (start us, length us, event | category | flops | bytes accessed | tf_op | source)
XLA Modules:
  0.0 92.6 jit_solution(10646085404228579079)
XLA Ops:
  0.6 9.7 %first_forward.1 = (bf16[36,2304]{1,0:T(8,128)(2,1)}, bf16[36,2304]{1,0:T(8,128)(2,1)}, bf16[36,2304]{1,0:T(8,128)(2,1)}, bf16[36,2304]{1,0:T(8,128)(2,1)}, s32[...) custom-call(bf16[144,144]{1,0:T(8,128)(2,1)} %constant.22.clone.refs_0_, ...), custom_call_target="tpu_custom_call" | custom-call | flops 1000000000 | bytes 4000000 | tf_op jit(solution)/shard_map/first_forward/pallas_call | solution.py:513
  10.3 4.9 %collective-permute-start = (bf16[36,2304]{1,0:T(8,128)(2,1)}, bf16[36,2304]{1,0:T(8,128)(2,1)S(1)}, u32[]{:S(2)}, u32[]{:S(2)}) collective-permute-start(bf16[36,2304]{1,0:T(8,128)(2,1)} %get-tuple-element.21), channel_id=1, source_target_pairs={{0,15},{1,0},{2,1},{3,2},{4,3},{5,4},{6,5},{7,6},{8,7},{9,8},{10,9... | collective-permute-start | bytes 497672 | tf_op jit(solution)/shard_map/ppermute | solution.py:538
  15.2 0.1 collective-permute-start.1
  15.3 5.7 %collective-permute-start.2 = (bf16[36,2304]{1,0:T(8,128)(2,1)}, bf16[36,2304]{1,0:T(8,128)(2,1)S(1)}, u32[]{:S(2)}, u32[]{:S(2)}) collective-permute-start(bf16[36,2304]{1,0:T(8,128)(2,1)} %get-tuple-element.23), channel_id=1, source_target_pairs={{0,127},{1,112},{2,113},{3,114},{4,115},{5,116},{6,117},{7,118},{8... | collective-permute-start | bytes 497672 | tf_op jit(solution)/shard_map/ppermute | solution.py:538
  21.0 6.5 %second_bias.1.refs_8_ = f32[24,144,144]{2,1,0:T(8,128)} custom-call(s32[6,2,12]{2,1,0:T(2,128)} %bitcast.27, s32[1]{0:T(128)} %bitcast.8.refs_1_, bf16[144,12]{1,0:T(8,128)(2,1)} %constant.25.clone.refs_2_, bf16[144,12]{1,0:T(8,128)(2,1)} %constant.26.clone.refs_3_, f32[2,24,759]{2,1,0:T(8,128)} %bitcast.25, s32[144,256]{1,0:T(8,128)} %get-tuple-element.24.refs_5_), custom_call_target="tpu_custom_call" | custom-call | flops 5000000000 | bytes 4000000 | tf_op jit(solution)/shard_map/second_bias/pallas_call | solution.py:513
  27.5 0.0 copy-start.3
  27.6 0.6 copy-done.2
  28.2 0.1 copy-done.3
  28.3 0.1 copy-done.4
  28.3 12.3 %second_block.1 = (bf16[36,1536]{1,0:T(8,128)(2,1)}, bf16[36,1536]{1,0:T(8,128)(2,1)}, bf16[36,1536]{1,0:T(8,128)(2,1)}, bf16[36,1536]{1,0:T(8,128)(2,1)}, bf16[...) custom-call(bf16[36,2304]{1,0:T(8,128)(2,1)} %get-tuple-element.20.refs_0_, bf16[36,2304]{1,0:T(8,128)(2,1)} %copy-done.2, ...), custom_call_target="tpu_custom_call" | custom-call | flops 15000000512 | bytes 4000000 | tf_op jit(solution)/shard_map/second_block/pallas_call | solution.py:513
  40.7 0.4 collective-permute-start.6
  41.0 0.1 collective-permute-start.4
  41.2 0.4 collective-permute-start.5
  41.5 1.6 %collective-permute-done.6.refs_1_ = bf16[144,2304]{1,0:T(8,128)(2,1)S(1)} collective-permute-done((bf16[144,2304]{1,0:T(8,128)(2,1)}, bf16[144,2304]{1,0:T(8,128)(2,1)S(1)}, u32[]{:S(2)}, u32[]{:S(2)}) %collective-permute-start.6) | collective-permute-done | bytes 663584 | tf_op jit(solution)/shard_map/ppermute | solution.py:560
  43.1 1.1 %copy-done.1 = bf16[144,2304]{1,0:T(8,128)(2,1)S(1)} copy-done((bf16[144,2304]{1,0:T(8,128)(2,1)S(1)}, bf16[144,2304]{1,0:T(8,128)(2,1)}, u32[]{:S(2)}) %copy-start.1) | copy-done | bytes 663576
  44.2 2.8 %weight_terms.1 = bf16[16,48,768]{2,1,0:T(8,128)(2,1)} custom-call(bf16[144,2304]{1,0:T(8,128)(2,1)S(1)} %copy-done.1, bf16[144,2304]{1,0:T(8,128)(2,1)S(1)} %collective-permute-done.6.refs_1_), custom_call_target="tpu_custom_call" | custom-call | flops 3000000000 | bytes 4000000 | tf_op jit(solution)/shard_map/weight_terms/pallas_call | solution.py:513
  47.0 4.4 %collective-permute-done.3.refs_0_ = bf16[36,1536]{1,0:T(8,128)(2,1)S(1)} collective-permute-done((bf16[36,1536]{1,0:T(8,128)(2,1)}, bf16[36,1536]{1,0:T(8,128)(2,1)S(1)}, u32[]{:S(2)}, u32[]{:S(2)}) %collective-permute-start.3) | collective-permute-done | bytes 110624 | tf_op jit(solution)/shard_map/ppermute | solution.py:538
  51.4 3.7 %all-to-all-start = ((bf16[16,48,768]{2,1,0:T(8,128)(2,1)}), bf16[16,48,768]{2,1,0:T(8,128)(2,1)S(1)}, u32[]{:S(2)}, u32[]{:S(2)}) async-start(bf16[16,48,768]{2,1,0:T(8,128)(2,1)} %weight_terms.1), calls=%async_computation | async-start | bytes 2359296 | tf_op jit(solution)/shard_map/all_to_all | solution.py:571
  55.2 8.9 %first_backward.1 = (bf16[72,2,768]{2,1,0:T(2,128)(2,1)}, bf16[72,2,768]{2,1,0:T(2,128)(2,1)}) custom-call(bf16[36,1536]{1,0:T(8,128)(2,1)} %copy-done.5, bf16[36,1536]{1,0:T(8,128)(2,1)} %copy-done.6, bf16[36,1536]{1,0:T(8,128)(2,1)} %copy-done.7, bf16[36,1536]{1,0:T(8,128)(2,1)} %get-tuple-element.28.refs_3_, bf16[144,768]{1,0:T(8,128)(2,1)} %get-tuple-element.29.refs_4_, ...), custom_call_target="tpu_custom_call" | custom-call | flops 8999999488 | bytes 4000000 | tf_op jit(solution)/shard_map/first_backward/pallas_call | solution.py:513
  64.1 9.8 %all-to-all-done.refs_0_ = bf16[16,48,768]{2,1,0:T(8,128)(2,1)S(1)} async-done(((bf16[16,48,768]{2,1,0:T(8,128)(2,1)}), bf16[16,48,768]{2,1,0:T(8,128)(2,1)S(1)}, u32[]{:S(2)}, u32[]{:S(2)}) %all-to-all-start) | async-done | bytes 1179680 | tf_op jit(solution)/shard_map/all_to_all | solution.py:571
  73.9 0.9 %copy-done = bf16[72,2,768]{2,1,0:T(2,128)(2,1)S(1)} copy-done((bf16[72,2,768]{2,1,0:T(2,128)(2,1)S(1)}, bf16[72,2,768]{2,1,0:T(2,128)(2,1)}, u32[]{:S(2)}) %copy-start) | copy-done | bytes 221208
  74.9 0.8 sum_plane.1
  75.6 15.9 %all_to_all.10.refs_0_ = bf16[16,48,128]{2,1,0:T(8,128)(2,1)S(1)} all-to-all(bf16[16,48,128]{2,1,0:T(8,128)(2,1)S(1)} %sum_plane.1), channel_id=1, replica_groups=mesh['member'=2,'lat'=8,'pair'=8,'core'=2] {'member','lat'}, dimensions={0} | all-to-all | bytes 393216 | tf_op jit(solution)/shard_map/all_to_all | solution.py:581
  91.6 0.9 sum_lat.1
  (16 shorter events, 0.0 us)
Async XLA Ops:
  10.3 17.2 %collective-permute-start = (bf16[36,2304]{1,0:T(8,128)(2,1)}, bf16[36,2304]{1,0:T(8,128)(2,1)S(1)}, u32[]{:S(2)}, u32[]{:S(2)}) collective-permute-start(bf16[36,2304]{1,0:T(8,128)(2,1)} %get-tuple-element.21), channel_id=1, source_target_pairs={{0,15},{1,0},{2,1},{3,2},{4,3},{5,4},{6,5},{7,6},{8,7},{9,8},{10,9... | collective-permute-start | bytes 497672 | tf_op jit(solution)/shard_map/ppermute | solution.py:538
  15.2 12.3 %collective-permute-start.1 = (bf16[36,2304]{1,0:T(8,128)(2,1)}, bf16[36,2304]{1,0:T(8,128)(2,1)S(1)}, u32[]{:S(2)}, u32[]{:S(2)}) collective-permute-start(bf16[36,2304]{1,0:T(8,128)(2,1)} %get-tuple-element.22), channel_id=1, source_target_pairs={{0,112},{1,113},{2,114},{3,115},{4,116},{5,117},{6,118},{7,119},{8... | collective-permute-start | bytes 497672 | tf_op jit(solution)/shard_map/ppermute | solution.py:538
  15.3 12.2 %collective-permute-start.2 = (bf16[36,2304]{1,0:T(8,128)(2,1)}, bf16[36,2304]{1,0:T(8,128)(2,1)S(1)}, u32[]{:S(2)}, u32[]{:S(2)}) collective-permute-start(bf16[36,2304]{1,0:T(8,128)(2,1)} %get-tuple-element.23), channel_id=1, source_target_pairs={{0,127},{1,112},{2,113},{3,114},{4,115},{5,116},{6,117},{7,118},{8... | collective-permute-start | bytes 497672 | tf_op jit(solution)/shard_map/ppermute | solution.py:538
  27.5 0.7 copy-start.2
  27.5 0.7 copy-start.3
  27.6 0.8 copy-start.4
  40.7 2.4 %collective-permute-start.6 = (bf16[144,2304]{1,0:T(8,128)(2,1)}, bf16[144,2304]{1,0:T(8,128)(2,1)S(1)}, u32[]{:S(2)}, u32[]{:S(2)}) collective-permute-start(bf16[144,2304]{1,0:T(8,128)(2,1)} %get-tuple-element.35), channel_id=1, source_target_pairs={{0,1},{1,0},{2,3},{3,2},{4,5},{5,4},{6,7},{7,6},{8,9},{9,8},{10,11... | collective-permute-start | bytes 1990664 | tf_op jit(solution)/shard_map/ppermute | solution.py:560
  41.0 10.4 %collective-permute-start.3 = (bf16[36,1536]{1,0:T(8,128)(2,1)}, bf16[36,1536]{1,0:T(8,128)(2,1)S(1)}, u32[]{:S(2)}, u32[]{:S(2)}) collective-permute-start(bf16[36,1536]{1,0:T(8,128)(2,1)} %get-tuple-element.25), channel_id=1, source_target_pairs={{0,17},{1,18},{2,19},{3,20},{4,21},{5,22},{6,23},{7,24},{8,25},{9,... | collective-permute-start | bytes 331784 | tf_op jit(solution)/shard_map/ppermute | solution.py:538
  41.0 10.4 %collective-permute-start.4 = (bf16[36,1536]{1,0:T(8,128)(2,1)}, bf16[36,1536]{1,0:T(8,128)(2,1)S(1)}, u32[]{:S(2)}, u32[]{:S(2)}) collective-permute-start(bf16[36,1536]{1,0:T(8,128)(2,1)} %get-tuple-element.26), channel_id=1, source_target_pairs={{0,16},{1,17},{2,18},{3,19},{4,20},{5,21},{6,22},{7,23},{8,24},{9,... | collective-permute-start | bytes 331784 | tf_op jit(solution)/shard_map/ppermute | solution.py:538
  41.2 10.2 %collective-permute-start.5 = (bf16[36,1536]{1,0:T(8,128)(2,1)}, bf16[36,1536]{1,0:T(8,128)(2,1)S(1)}, u32[]{:S(2)}, u32[]{:S(2)}) collective-permute-start(bf16[36,1536]{1,0:T(8,128)(2,1)} %get-tuple-element.27), channel_id=1, source_target_pairs={{0,1},{1,2},{2,3},{3,4},{4,5},{5,6},{6,7},{7,8},{8,9},{9,10},{10,1... | collective-permute-start | bytes 331784 | tf_op jit(solution)/shard_map/ppermute | solution.py:538
  43.1 1.1 %copy-start.1 = (bf16[144,2304]{1,0:T(8,128)(2,1)S(1)}, bf16[144,2304]{1,0:T(8,128)(2,1)}, u32[]{:S(2)}) copy-start(bf16[144,2304]{1,0:T(8,128)(2,1)} %get-tuple-element.34.refs_0_) | copy-start | bytes 1990660
  51.4 3.7 %copy-start.5 = (bf16[36,1536]{1,0:T(8,128)(2,1)}, bf16[36,1536]{1,0:T(8,128)(2,1)S(1)}, u32[]{:S(2)}) copy-start(bf16[36,1536]{1,0:T(8,128)(2,1)S(1)} %collective-permute-done.3.refs_0_) | copy-start | bytes 331780
  51.4 3.7 %copy-start.6 = (bf16[36,1536]{1,0:T(8,128)(2,1)}, bf16[36,1536]{1,0:T(8,128)(2,1)S(1)}, u32[]{:S(2)}) copy-start(bf16[36,1536]{1,0:T(8,128)(2,1)S(1)} %collective-permute-done.4.refs_1_) | copy-start | bytes 331780
  51.4 3.8 %copy-start.7 = (bf16[36,1536]{1,0:T(8,128)(2,1)}, bf16[36,1536]{1,0:T(8,128)(2,1)S(1)}, u32[]{:S(2)}) copy-start(bf16[36,1536]{1,0:T(8,128)(2,1)S(1)} %collective-permute-done.5.refs_2_) | copy-start | bytes 331780
  51.4 22.5 %all-to-all-start = ((bf16[16,48,768]{2,1,0:T(8,128)(2,1)}), bf16[16,48,768]{2,1,0:T(8,128)(2,1)S(1)}, u32[]{:S(2)}, u32[]{:S(2)}) async-start(bf16[16,48,768]{2,1,0:T(8,128)(2,1)} %weight_terms.1), calls=%async_computation | async-start | bytes 2359296 | tf_op jit(solution)/shard_map/all_to_all | solution.py:571
  73.9 0.9 %copy-start = (bf16[72,2,768]{2,1,0:T(2,128)(2,1)S(1)}, bf16[72,2,768]{2,1,0:T(2,128)(2,1)}, u32[]{:S(2)}) copy-start(bf16[72,2,768]{2,1,0:T(2,128)(2,1)} %get-tuple-element.33.refs_1_) | copy-start | bytes 663556
where the time goes:
time: 92.9 us; the launch traced here: 92.6 us
  Pallas kernels  41.9 us (45%)
  blocking collectives  15.9 us (17%)
  waiting for transfers between devices  15.8 us (17%)
  starting transfers between devices  15.3 us (16%)
  local copies, waits for them, and re-layouts  2.79 us (3%)
  between operations  0.97 us (1%)
    pallas_call x7, Pallas kernels, call(): pl.pallas_call(run, out_shape=[jax.ShapeDtypeStruct(shape, kind) for shap...  41.9 us
    all_to_all x1, blocking collectives, reduce_terms(): parts = lax.all_to_all(plane_sum, ('member', 'lat'), 0, 0, tiled=True)  15.9 us
    ppermute x6, starting transfers between devices, moved(): return lax.ppermute(shard, ('lat', 'pair', 'core'), pairs)  11.2 us
    all_to_all x1, waiting for transfers between devices, reduce_terms(): parts = lax.all_to_all(terms, ('member', 'pair'), 0, 0, tiled=True)  9.82 us
    ppermute x6, waiting for transfers between devices, moved(): return lax.ppermute(shard, ('lat', 'pair', 'core'), pairs)  4.42 us
    all_to_all x1, starting transfers between devices, reduce_terms(): parts = lax.all_to_all(terms, ('member', 'pair'), 0, 0, tiled=True)  3.71 us
    unnamed x16, local copies, waits for them, and re-layouts  2.79 us
  transfers between devices with their start and end apart: 8, of which 3 were waited for; matrix products, arithmetic and copies ran while one was open for 0% of the time, Pallas kernels for 20%

commit v1 on v0

--- a/solution.py
+++ b/solution.py
@@ -308,7 +308,14 @@
         blocks.put(quad)
 
 
-def second_bias(blocks, rows_ref, tail_ref, mask_ref, sems):
+def pick_columns(core, width):
+    rows = lax.broadcasted_iota(jnp.int32, (D // 2, D), 0)
+    cols = lax.broadcasted_iota(jnp.int32, (D // 2, D), 1)
+    part = jnp.floor((rows.astype(f32) + 0.5) * (1.0 / width)).astype(jnp.int32)
+    return (cols == rows + width * (part + core)).astype(f32).astype(bf16)
+
+
+def second_bias(width, blocks, rows_ref, tail_ref, mask_ref, sems):
     region_ref, edge_ref, bias_ref = blocks.get(0), blocks.get(1), blocks.outs[0]
     labels = jnp.concatenate([region_ref[row] for row in range(WIN_LAT)], axis=0)
     labels = labels.astype(f32) * 2.0 - 1.0
@@ -327,18 +334,16 @@
         rows = pl.ds(third * (WIN // 3), WIN // 3)
         blocks.put(0, (slice(None), rows), sems.at[third])
 
+    core = blocks.get(6)[0]
+    blocks.outs[1][0] = pick_columns(core, width)
+    blocks.outs[1][1] = pick_columns(1 - core, width)
+    blocks.put(1)
     gather_bias(blocks.get(5), blocks.get(4), bias_ref, rows_ref, tail_ref, mask_ref, done)
 
 
-def pick_columns(core, width):
-    rows = lax.broadcasted_iota(jnp.int32, (D // 2, D), 0)
-    cols = lax.broadcasted_iota(jnp.int32, (D // 2, D), 1)
-    part = jnp.floor((rows.astype(f32) + 0.5) * (1.0 / width)).astype(jnp.int32)
-    return (cols == rows + width * (part + core)).astype(f32).astype(bf16)
-
-
 def second_block(
-    width, blocks, hold_ref, mixed_ref, qkv_ref, probs_ref, grad_mixed_ref, turned_ref, grad_rows_ref
+    blocks, hold_ref, mixed_ref, qkv_ref, probs_ref, grad_mixed_ref, turned_ref, grad_rows_ref,
+    sems,
 ):
     leaving = blocks.outs[:4]
     own_ref, other_ref = blocks.outs[4:]
@@ -356,28 +361,34 @@
     w_out_ref = blocks.get(9)
     result = values_f + mm(mixed_ref[...], w_out_ref[...])
     put_quads(result, hold_ref, leaving, 1)
+    for quad in range(4):
+        blocks.put(quad, (slice(None), pl.ds(D, D)), sems.at[quad])
     grad_f = take_quads(arrived, hold_ref, 1)
     grad = grad_f.astype(bf16)
     first_mixed = take_quads(arrived, hold_ref, 2).astype(bf16)
     half = D // 2
-    core = blocks.get(10)[0]
-    own, other = pick_columns(core, width), pick_columns(1 - core, width)
+    own, other = blocks.get(10)[0], blocks.get(10)[1]
     for ref, pick in ((own_ref, own), (other_ref, other)):
         ref[:, :D] = first_mixed
         ref[:, D : 2 * D] = mixed_ref[...]
         ref[:, 2 * D + half :] = mm_t(grad, pick).astype(bf16)
+    early = ((0, 2 * D), (2 * D + half, half))
+    for place in (4, 5):
+        for part, (start, size) in enumerate(early):
+            blocks.put(place, (slice(None), pl.ds(start, size)), sems.at[2 * place - 4 + part])
     back_attend(
         grad, qkv_ref, probs_ref, mixed_ref, w_out_ref, grad_mixed_ref, turned_ref, grad_rows_ref
     )
     grad_input = back_norm(grad_f, normed, inv_std, gain, grad_rows_ref, w_parts)
     first_grad = grad_input.astype(bf16)
     other_ref[:, 2 * D : 2 * D + half] = mm_t(first_grad, other).astype(bf16)
-    blocks.put(5)
+    late = (slice(None), pl.ds(2 * D, half))
+    blocks.put(5, late)
     put_quads(grad_input, hold_ref, leaving, 0)
     for quad in range(4):
-        blocks.put(quad)
+        blocks.put(quad, (slice(None), pl.ds(0, D)))
     own_ref[:, 2 * D : 2 * D + half] = mm_t(first_grad, own).astype(bf16)
-    blocks.put(4)
+    blocks.put(4, late)
 
 
 def weight_terms(blocks, sems):
@@ -597,9 +608,9 @@
     back_order = jnp.asarray(order.T, bf16)
     order = jnp.asarray(order, bf16)
     at_line, at_col = jnp.asarray(at_line, bf16), jnp.asarray(at_col, bf16)
-    edge = (lax.axis_index("lat") == lax.axis_size("lat") - 1).astype(jnp.int32).reshape(1)
+    edge = (lax.axis_index("lat") == lax.axis_size("lat") - 1).astype(jnp.int32)
     n_pair, n_core = lax.axis_size("pair"), lax.axis_size("core")
-    core = lax.axis_index("core")
+    core = lax.axis_index("core").astype(jnp.int32)
 
     def qkv_parts(block):
         def part_of(part):
@@ -643,34 +654,36 @@
     )
     wide, inputs, qkv_one, probs_one = first[4:]
     shifted = exchange(first[:4], True)
-    (bias_two,) = call(
-        second_bias,
+    bias_two, picks = call(
+        functools.partial(second_bias, D // (n_pair * n_core)),
         [
             (region.transpose(1, 0, 2), HBM, None),
-            (edge, SMEM, None),
+            (edge.reshape(1), SMEM, None),
             (at_line, HBM, None),
             (at_col, HBM, None),
             (table, HBM, 1),
             (wide, HBM, None),
+            (core.reshape(1), SMEM, None),
         ],
-        [((HEADS, WIN, WIN), f32, HBM)],
+        [((HEADS, WIN, WIN), f32, HBM), ((2, D // 2, D), bf16, HBM)],
         gather_scratch + [pltpu.VMEM((WIN, WIN), f32), pltpu.SemaphoreType.DMA((3,))],
         5_000_000_000,
         "second_bias",
     )
     second = call(
-        functools.partial(second_block, D // (n_pair * n_core)),
+        second_block,
         [(quad, HBM, None) for quad in shifted]
         + [
             (norm_gain, HBM, None),
             *qkv_parts(1),
             (bias_two, HBM, None),
             (out_weight, HBM, 1),
-            (core.astype(jnp.int32).reshape(1), SMEM, None),
+            (picks, HBM, None),
         ],
         [((QUAD, 2 * D), bf16, HBM)] * 4 + [((WIN, 3 * D), bf16, HBM)] * 2,
         [hold, mixed_scratch, pltpu.VMEM((WIN, 3 * D), bf16), pltpu.VMEM((HEADS, WIN, WIN), bf16)]
-        + back_scratch,
+        + back_scratch
+        + [pltpu.SemaphoreType.DMA((8,))],
         15_000_000_000,
         "second_block",
     )

time: 92.9 us -> 92.7 us (level)
  no operation moved by 1% of the time
where the time goes in v1:
time: 92.7 us; the launch traced here: 92.4 us
  Pallas kernels  42.1 us (45%)
  blocking collectives  16 us (17%)
  starting transfers between devices  15.3 us (17%)
  waiting for transfers between devices  15.2 us (16%)
  local copies, waits for them, and re-layouts  2.79 us (3%)
  between operations  0.97 us (1%)
    pallas_call x7, Pallas kernels, call(): pl.pallas_call(run, out_shape=[jax.ShapeDtypeStruct(shape, kind) for shap...  42.1 us
    all_to_all x1, blocking collectives, reduce_terms(): parts = lax.all_to_all(plane_sum, ('member', 'lat'), 0, 0, tiled=True)  16 us
    ppermute x6, starting transfers between devices, moved(): return lax.ppermute(shard, ('lat', 'pair', 'core'), pairs)  11.2 us
    all_to_all x1, waiting for transfers between devices, reduce_terms(): parts = lax.all_to_all(terms, ('member', 'pair'), 0, 0, tiled=True)  9.72 us
    ppermute x6, waiting for transfers between devices, moved(): return lax.ppermute(shard, ('lat', 'pair', 'core'), pairs)  3.98 us
    all_to_all x1, starting transfers between devices, reduce_terms(): parts = lax.all_to_all(terms, ('member', 'pair'), 0, 0, tiled=True)  3.71 us
    unnamed x16, local copies, waits for them, and re-layouts  2.79 us
  transfers between devices with their start and end apart: 8, of which 3 were waited for; matrix products, arithmetic and copies ran while one was open for 0% of the time, Pallas kernels for 20%

profile of v1, /device:TPU:32, one launch (start us, length us, event | category | flops | bytes accessed | tf_op | source)
XLA Modules:
  0.0 92.4 jit_solution(3845300509984654492)
XLA Ops:
  0.6 9.7 %first_forward.1 = (bf16[36,2304]{1,0:T(8,128)(2,1)}, bf16[36,2304]{1,0:T(8,128)(2,1)}, bf16[36,2304]{1,0:T(8,128)(2,1)}, bf16[36,2304]{1,0:T(8,128)(2,1)}, s32[...) custom-call(bf16[144,144]{1,0:T(8,128)(2,1)} %constant.22.clone.refs_0_, ...), custom_call_target="tpu_custom_call" | custom-call | flops 1000000000 | bytes 4000000 | tf_op jit(solution)/shard_map/first_forward/pallas_call | solution.py:524
  10.3 4.9 %collective-permute-start = (bf16[36,2304]{1,0:T(8,128)(2,1)}, bf16[36,2304]{1,0:T(8,128)(2,1)S(1)}, u32[]{:S(2)}, u32[]{:S(2)}) collective-permute-start(bf16[36,2304]{1,0:T(8,128)(2,1)} %get-tuple-element.23), channel_id=1, source_target_pairs={{0,15},{1,0},{2,1},{3,2},{4,3},{5,4},{6,5},{7,6},{8,7},{9,8},{10,9... | collective-permute-start | bytes 497672 | tf_op jit(solution)/shard_map/ppermute | solution.py:549
  15.2 0.1 collective-permute-start.1
  15.3 5.7 %collective-permute-start.2 = (bf16[36,2304]{1,0:T(8,128)(2,1)}, bf16[36,2304]{1,0:T(8,128)(2,1)S(1)}, u32[]{:S(2)}, u32[]{:S(2)}) collective-permute-start(bf16[36,2304]{1,0:T(8,128)(2,1)} %get-tuple-element.25), channel_id=1, source_target_pairs={{0,127},{1,112},{2,113},{3,114},{4,115},{5,116},{6,117},{7,118},{8... | collective-permute-start | bytes 497672 | tf_op jit(solution)/shard_map/ppermute | solution.py:549
  21.0 7.0 %second_bias.1 = (f32[24,144,144]{2,1,0:T(8,128)}, bf16[2,384,768]{2,1,0:T(8,128)(2,1)}) custom-call(s32[6,2,12]{2,1,0:T(2,128)} %bitcast.27, s32[1]{0:T(128)} %bitcast.8.refs_1_, bf16[144,12]{1,0:T(8,128)(2,1)} %constant.25.clone.refs_2_, bf16[144,12]{1,0:T(8,128)(2,1)} %constant.26.clone.refs_3_, f32[2,24,759]{2,1,0:T(8,128)} %bitcast.25, ...), custom_call_target="tpu_custom_call" | custom-call | flops 5000000000 | bytes 4000000 | tf_op jit(solution)/shard_map/second_bias/pallas_call | solution.py:524
  28.1 0.0 copy-start.3
  28.1 0.6 copy-done.2
  28.7 0.0 copy-done.3
  28.8 0.1 copy-done.4
  28.8 12.1 %second_block.1 = (bf16[36,1536]{1,0:T(8,128)(2,1)}, bf16[36,1536]{1,0:T(8,128)(2,1)}, bf16[36,1536]{1,0:T(8,128)(2,1)}, bf16[36,1536]{1,0:T(8,128)(2,1)}, bf16[...) custom-call(bf16[36,2304]{1,0:T(8,128)(2,1)} %get-tuple-element.22.refs_0_, bf16[36,2304]{1,0:T(8,128)(2,1)} %copy-done.2, ...), custom_call_target="tpu_custom_call" | custom-call | flops 15000000512 | bytes 4000000 | tf_op jit(solution)/shard_map/second_block/pallas_call | solution.py:524
  40.9 0.4 collective-permute-start.6
  41.3 0.1 collective-permute-start.4
  41.4 0.4 collective-permute-start.5
  41.8 1.5 %collective-permute-done.6.refs_1_ = bf16[144,2304]{1,0:T(8,128)(2,1)S(1)} collective-permute-done((bf16[144,2304]{1,0:T(8,128)(2,1)}, bf16[144,2304]{1,0:T(8,128)(2,1)S(1)}, u32[]{:S(2)}, u32[]{:S(2)}) %collective-permute-start.6) | collective-permute-done | bytes 663584 | tf_op jit(solution)/shard_map/ppermute | solution.py:571
  43.3 1.1 %copy-done.1 = bf16[144,2304]{1,0:T(8,128)(2,1)S(1)} copy-done((bf16[144,2304]{1,0:T(8,128)(2,1)S(1)}, bf16[144,2304]{1,0:T(8,128)(2,1)}, u32[]{:S(2)}) %copy-start.1) | copy-done | bytes 663576
  44.4 2.8 %weight_terms.1 = bf16[16,48,768]{2,1,0:T(8,128)(2,1)} custom-call(bf16[144,2304]{1,0:T(8,128)(2,1)S(1)} %copy-done.1, bf16[144,2304]{1,0:T(8,128)(2,1)S(1)} %collective-permute-done.6.refs_1_), custom_call_target="tpu_custom_call" | custom-call | flops 3000000000 | bytes 4000000 | tf_op jit(solution)/shard_map/weight_terms/pallas_call | solution.py:524
  47.2 4.0 %collective-permute-done.3.refs_0_ = bf16[36,1536]{1,0:T(8,128)(2,1)S(1)} collective-permute-done((bf16[36,1536]{1,0:T(8,128)(2,1)}, bf16[36,1536]{1,0:T(8,128)(2,1)S(1)}, u32[]{:S(2)}, u32[]{:S(2)}) %collective-permute-start.3) | collective-permute-done | bytes 110624 | tf_op jit(solution)/shard_map/ppermute | solution.py:549
  51.2 3.7 %all-to-all-start = ((bf16[16,48,768]{2,1,0:T(8,128)(2,1)}), bf16[16,48,768]{2,1,0:T(8,128)(2,1)S(1)}, u32[]{:S(2)}, u32[]{:S(2)}) async-start(bf16[16,48,768]{2,1,0:T(8,128)(2,1)} %weight_terms.1), calls=%async_computation | async-start | bytes 2359296 | tf_op jit(solution)/shard_map/all_to_all | solution.py:582
  55.0 8.9 %first_backward.1 = (bf16[72,2,768]{2,1,0:T(2,128)(2,1)}, bf16[72,2,768]{2,1,0:T(2,128)(2,1)}) custom-call(bf16[36,1536]{1,0:T(8,128)(2,1)} %copy-done.5, bf16[36,1536]{1,0:T(8,128)(2,1)} %copy-done.6, bf16[36,1536]{1,0:T(8,128)(2,1)} %copy-done.7, bf16[36,1536]{1,0:T(8,128)(2,1)} %get-tuple-element.32.refs_3_, bf16[144,768]{1,0:T(8,128)(2,1)} %get-tuple-element.33.refs_4_, ...), custom_call_target="tpu_custom_call" | custom-call | flops 8999999488 | bytes 4000000 | tf_op jit(solution)/shard_map/first_backward/pallas_call | solution.py:524
  63.9 9.7 %all-to-all-done.refs_0_ = bf16[16,48,768]{2,1,0:T(8,128)(2,1)S(1)} async-done(((bf16[16,48,768]{2,1,0:T(8,128)(2,1)}), bf16[16,48,768]{2,1,0:T(8,128)(2,1)S(1)}, u32[]{:S(2)}, u32[]{:S(2)}) %all-to-all-start) | async-done | bytes 1179680 | tf_op jit(solution)/shard_map/all_to_all | solution.py:582
  73.6 0.9 %copy-done = bf16[72,2,768]{2,1,0:T(2,128)(2,1)S(1)} copy-done((bf16[72,2,768]{2,1,0:T(2,128)(2,1)S(1)}, bf16[72,2,768]{2,1,0:T(2,128)(2,1)}, u32[]{:S(2)}) %copy-start) | copy-done | bytes 221208
  74.6 0.8 sum_plane.1
  75.3 16.0 %all_to_all.10.refs_0_ = bf16[16,48,128]{2,1,0:T(8,128)(2,1)S(1)} all-to-all(bf16[16,48,128]{2,1,0:T(8,128)(2,1)S(1)} %sum_plane.1), channel_id=1, replica_groups=mesh['member'=2,'lat'=8,'pair'=8,'core'=2] {'member','lat'}, dimensions={0} | all-to-all | bytes 393216 | tf_op jit(solution)/shard_map/all_to_all | solution.py:592
  91.3 0.9 sum_lat.1
  (16 shorter events, 0.0 us)
Async XLA Ops:
  10.3 17.7 %collective-permute-start = (bf16[36,2304]{1,0:T(8,128)(2,1)}, bf16[36,2304]{1,0:T(8,128)(2,1)S(1)}, u32[]{:S(2)}, u32[]{:S(2)}) collective-permute-start(bf16[36,2304]{1,0:T(8,128)(2,1)} %get-tuple-element.23), channel_id=1, source_target_pairs={{0,15},{1,0},{2,1},{3,2},{4,3},{5,4},{6,5},{7,6},{8,7},{9,8},{10,9... | collective-permute-start | bytes 497672 | tf_op jit(solution)/shard_map/ppermute | solution.py:549
  15.2 12.8 %collective-permute-start.1 = (bf16[36,2304]{1,0:T(8,128)(2,1)}, bf16[36,2304]{1,0:T(8,128)(2,1)S(1)}, u32[]{:S(2)}, u32[]{:S(2)}) collective-permute-start(bf16[36,2304]{1,0:T(8,128)(2,1)} %get-tuple-element.24), channel_id=1, source_target_pairs={{0,112},{1,113},{2,114},{3,115},{4,116},{5,117},{6,118},{7,119},{8... | collective-permute-start | bytes 497672 | tf_op jit(solution)/shard_map/ppermute | solution.py:549
  15.3 12.8 %collective-permute-start.2 = (bf16[36,2304]{1,0:T(8,128)(2,1)}, bf16[36,2304]{1,0:T(8,128)(2,1)S(1)}, u32[]{:S(2)}, u32[]{:S(2)}) collective-permute-start(bf16[36,2304]{1,0:T(8,128)(2,1)} %get-tuple-element.25), channel_id=1, source_target_pairs={{0,127},{1,112},{2,113},{3,114},{4,115},{5,116},{6,117},{7,118},{8... | collective-permute-start | bytes 497672 | tf_op jit(solution)/shard_map/ppermute | solution.py:549
  28.0 0.7 copy-start.2
  28.1 0.7 copy-start.3
  28.1 0.8 copy-start.4
  40.9 2.4 %collective-permute-start.6 = (bf16[144,2304]{1,0:T(8,128)(2,1)}, bf16[144,2304]{1,0:T(8,128)(2,1)S(1)}, u32[]{:S(2)}, u32[]{:S(2)}) collective-permute-start(bf16[144,2304]{1,0:T(8,128)(2,1)} %get-tuple-element.39), channel_id=1, source_target_pairs={{0,1},{1,0},{2,3},{3,2},{4,5},{5,4},{6,7},{7,6},{8,9},{9,8},{10,11... | collective-permute-start | bytes 1990664 | tf_op jit(solution)/shard_map/ppermute | solution.py:571
  41.3 9.9 %collective-permute-start.3 = (bf16[36,1536]{1,0:T(8,128)(2,1)}, bf16[36,1536]{1,0:T(8,128)(2,1)S(1)}, u32[]{:S(2)}, u32[]{:S(2)}) collective-permute-start(bf16[36,1536]{1,0:T(8,128)(2,1)} %get-tuple-element.29), channel_id=1, source_target_pairs={{0,17},{1,18},{2,19},{3,20},{4,21},{5,22},{6,23},{7,24},{8,25},{9,... | collective-permute-start | bytes 331784 | tf_op jit(solution)/shard_map/ppermute | solution.py:549
  41.3 9.9 %collective-permute-start.4 = (bf16[36,1536]{1,0:T(8,128)(2,1)}, bf16[36,1536]{1,0:T(8,128)(2,1)S(1)}, u32[]{:S(2)}, u32[]{:S(2)}) collective-permute-start(bf16[36,1536]{1,0:T(8,128)(2,1)} %get-tuple-element.30), channel_id=1, source_target_pairs={{0,16},{1,17},{2,18},{3,19},{4,20},{5,21},{6,22},{7,23},{8,24},{9,... | collective-permute-start | bytes 331784 | tf_op jit(solution)/shard_map/ppermute | solution.py:549
  41.4 9.8 %collective-permute-start.5 = (bf16[36,1536]{1,0:T(8,128)(2,1)}, bf16[36,1536]{1,0:T(8,128)(2,1)S(1)}, u32[]{:S(2)}, u32[]{:S(2)}) collective-permute-start(bf16[36,1536]{1,0:T(8,128)(2,1)} %get-tuple-element.31), channel_id=1, source_target_pairs={{0,1},{1,2},{2,3},{3,4},{4,5},{5,6},{6,7},{7,8},{8,9},{9,10},{10,1... | collective-permute-start | bytes 331784 | tf_op jit(solution)/shard_map/ppermute | solution.py:549
  43.3 1.1 %copy-start.1 = (bf16[144,2304]{1,0:T(8,128)(2,1)S(1)}, bf16[144,2304]{1,0:T(8,128)(2,1)}, u32[]{:S(2)}) copy-start(bf16[144,2304]{1,0:T(8,128)(2,1)} %get-tuple-element.38.refs_0_) | copy-start | bytes 1990660
  51.2 3.7 %copy-start.5 = (bf16[36,1536]{1,0:T(8,128)(2,1)}, bf16[36,1536]{1,0:T(8,128)(2,1)S(1)}, u32[]{:S(2)}) copy-start(bf16[36,1536]{1,0:T(8,128)(2,1)S(1)} %collective-permute-done.3.refs_0_) | copy-start | bytes 331780
  51.2 3.7 %copy-start.6 = (bf16[36,1536]{1,0:T(8,128)(2,1)}, bf16[36,1536]{1,0:T(8,128)(2,1)S(1)}, u32[]{:S(2)}) copy-start(bf16[36,1536]{1,0:T(8,128)(2,1)S(1)} %collective-permute-done.4.refs_1_) | copy-start | bytes 331780
  51.2 3.8 %copy-start.7 = (bf16[36,1536]{1,0:T(8,128)(2,1)}, bf16[36,1536]{1,0:T(8,128)(2,1)S(1)}, u32[]{:S(2)}) copy-start(bf16[36,1536]{1,0:T(8,128)(2,1)S(1)} %collective-permute-done.5.refs_2_) | copy-start | bytes 331780
  51.2 22.4 %all-to-all-start = ((bf16[16,48,768]{2,1,0:T(8,128)(2,1)}), bf16[16,48,768]{2,1,0:T(8,128)(2,1)S(1)}, u32[]{:S(2)}, u32[]{:S(2)}) async-start(bf16[16,48,768]{2,1,0:T(8,128)(2,1)} %weight_terms.1), calls=%async_computation | async-start | bytes 2359296 | tf_op jit(solution)/shard_map/all_to_all | solution.py:582
  73.6 0.9 %copy-start = (bf16[72,2,768]{2,1,0:T(2,128)(2,1)S(1)}, bf16[72,2,768]{2,1,0:T(2,128)(2,1)}, u32[]{:S(2)}) copy-start(bf16[72,2,768]{2,1,0:T(2,128)(2,1)} %get-tuple-element.37.refs_1_) | copy-start | bytes 663556

commit v2 on v1

--- a/solution.py
+++ b/solution.py
@@ -193,7 +193,7 @@
     return slice(part * D + group * 128, part * D + (group + 1) * 128)
 
 
-def attend(qkv_ref, bias_ref, probs_ref, mixed_ref):
+def attend(qkv_ref, bias_ref, probs_ref, mixed_ref, beside=None):
     masks = head_masks()
     ones = jnp.ones((WIN, 128), bf16)
     for group in range(GROUPS):
@@ -210,18 +210,22 @@
         probs_ref[heads] = weights.astype(bf16).reshape(GROUP, WIN, WIN)
         mixed = merge_heads(product[:, :128] * share)
         mixed_ref[:, group_cols(group, 0)] = mixed.astype(bf16)
-
-
-def back_attend(grad, qkv_ref, probs_ref, mixed_ref, w_out_ref, grad_mixed_ref, turned_ref, rows_ref):
+        if beside is not None:
+            beside(group)
+
+
+def prepare_back(part, grad, qkv_ref, w_out_ref, grad_mixed_ref, turned_ref):
+    unit = eye(256)
+    cols = slice(part * 256, (part + 1) * 256)
+    grad_mixed_ref[:, cols] = mm_t(grad, w_out_ref[cols, :]).astype(bf16)
+    turned_ref[0, cols, :] = mm_t(unit, grad_mixed_ref[:, cols]).astype(bf16)
+    turned_ref[1, cols, :] = mm_t(unit, qkv_ref[:, cols]).astype(bf16)
+
+
+def back_attend(qkv_ref, probs_ref, mixed_ref, grad_mixed_ref, turned_ref, rows_ref, beside=None):
     masks = head_masks()
-    unit = eye(256)
     small = eye(WIN)
     minus = -jnp.ones((WIN, 128), bf16)
-    grad_mixed_ref[...] = mm_t(grad, w_out_ref[...]).astype(bf16)
-    for part in range(3):
-        cols = slice(part * 256, (part + 1) * 256)
-        turned_ref[0, cols, :] = mm_t(unit, grad_mixed_ref[:, cols]).astype(bf16)
-        turned_ref[1, cols, :] = mm_t(unit, qkv_ref[:, cols]).astype(bf16)
     for group in range(GROUPS):
         heads = slice(group * GROUP, (group + 1) * GROUP)
         cols = group_cols(group, 0)
@@ -246,6 +250,8 @@
             tokens = slice(inner * WIN, (inner + 1) * WIN)
             turned_ref[2, lines, :] = mm(turned_ref[1, lines, :], grad_scores[tokens]).astype(bf16)
             turned_ref[3, lines, :] = mm(turned_ref[0, lines, :], weights[tokens]).astype(bf16)
+        if beside is not None:
+            beside(group)
     for part in range(3):
         cols = slice(part * 256, (part + 1) * 256)
         for which in (1, 2):
@@ -315,7 +321,7 @@
     return (cols == rows + width * (part + core)).astype(f32).astype(bf16)
 
 
-def second_bias(width, blocks, rows_ref, tail_ref, mask_ref, sems):
+def second_bias(width, blocks, rows_ref, tail_ref, mask_ref):
     region_ref, edge_ref, bias_ref = blocks.get(0), blocks.get(1), blocks.outs[0]
     labels = jnp.concatenate([region_ref[row] for row in range(WIN_LAT)], axis=0)
     labels = labels.astype(f32) * 2.0 - 1.0
@@ -330,15 +336,10 @@
     allowed = jnp.logical_and(same, jnp.logical_not(across))
     mask_ref[...] = jnp.where(allowed, 0.0, -jnp.inf)
 
-    def done(third):
-        rows = pl.ds(third * (WIN // 3), WIN // 3)
-        blocks.put(0, (slice(None), rows), sems.at[third])
-
     core = blocks.get(6)[0]
     blocks.outs[1][0] = pick_columns(core, width)
     blocks.outs[1][1] = pick_columns(1 - core, width)
-    blocks.put(1)
-    gather_bias(blocks.get(5), blocks.get(4), bias_ref, rows_ref, tail_ref, mask_ref, done)
+    gather_bias(blocks.get(5), blocks.get(4), bias_ref, rows_ref, tail_ref, mask_ref)
 
 
 def second_block(
@@ -354,40 +355,52 @@
     hidden = (normed * gain).astype(bf16)
 
     def w_parts(part):
-        return blocks.get(5 + part)
+        return blocks.get(5).at[1, :, pl.ds(part * D, D)]
 
     project_qkv(hidden, w_parts, qkv_ref)
-    attend(qkv_ref, blocks.get(8), probs_ref, mixed_ref)
-    w_out_ref = blocks.get(9)
-    result = values_f + mm(mixed_ref[...], w_out_ref[...])
-    put_quads(result, hold_ref, leaving, 1)
-    for quad in range(4):
-        blocks.put(quad, (slice(None), pl.ds(D, D)), sems.at[quad])
     grad_f = take_quads(arrived, hold_ref, 1)
     grad = grad_f.astype(bf16)
     first_mixed = take_quads(arrived, hold_ref, 2).astype(bf16)
     half = D // 2
-    own, other = blocks.get(10)[0], blocks.get(10)[1]
-    for ref, pick in ((own_ref, own), (other_ref, other)):
-        ref[:, :D] = first_mixed
+    bias_ref, w_out_ref, picks_ref = blocks.get(7), blocks.get(6).at[1], blocks.get(8)
+
+    def beside_forward(group):
+        if group < 3:
+            prepare_back(group, grad, qkv_ref, w_out_ref, grad_mixed_ref, turned_ref)
+        elif group < 5:
+            ref = (own_ref, other_ref)[group - 3]
+            ref[:, :D] = first_mixed
+            ref[:, 2 * D + half :] = mm_t(grad, picks_ref[group - 3]).astype(bf16)
+
+    attend(qkv_ref, bias_ref, probs_ref, mixed_ref, beside_forward)
+    early = ((0, 2 * D), (2 * D + half, half))
+    for place, ref in ((4, own_ref), (5, other_ref)):
         ref[:, D : 2 * D] = mixed_ref[...]
-        ref[:, 2 * D + half :] = mm_t(grad, pick).astype(bf16)
-    early = ((0, 2 * D), (2 * D + half, half))
-    for place in (4, 5):
         for part, (start, size) in enumerate(early):
             blocks.put(place, (slice(None), pl.ds(start, size)), sems.at[2 * place - 4 + part])
+
+    def beside_back(group):
+        if group < 3:
+            cols = slice(group * 256, (group + 1) * 256)
+            hold_ref[:, cols] = values_f[:, cols] + mm(mixed_ref[...], w_out_ref[:, cols])
+        elif group == 3:
+            for quad in range(4):
+                rows = slice(quad * QUAD, (quad + 1) * QUAD)
+                leaving[quad][:, D:] = hold_ref[rows, :].astype(bf16)
+                blocks.put(quad, (slice(None), pl.ds(D, D)), sems.at[quad])
+
     back_attend(
-        grad, qkv_ref, probs_ref, mixed_ref, w_out_ref, grad_mixed_ref, turned_ref, grad_rows_ref
+        qkv_ref, probs_ref, mixed_ref, grad_mixed_ref, turned_ref, grad_rows_ref, beside_back
     )
     grad_input = back_norm(grad_f, normed, inv_std, gain, grad_rows_ref, w_parts)
     first_grad = grad_input.astype(bf16)
-    other_ref[:, 2 * D : 2 * D + half] = mm_t(first_grad, other).astype(bf16)
+    other_ref[:, 2 * D : 2 * D + half] = mm_t(first_grad, picks_ref[1]).astype(bf16)
     late = (slice(None), pl.ds(2 * D, half))
     blocks.put(5, late)
     put_quads(grad_input, hold_ref, leaving, 0)
     for quad in range(4):
         blocks.put(quad, (slice(None), pl.ds(0, D)))
-    own_ref[:, 2 * D : 2 * D + half] = mm_t(first_grad, own).astype(bf16)
+    own_ref[:, 2 * D : 2 * D + half] = mm_t(first_grad, picks_ref[0]).astype(bf16)
     blocks.put(4, late)
 
 
@@ -422,7 +435,6 @@
         piece = total[:, place * width : (place + 1) * width].astype(bf16)
         for copy in range(copies):
             out_ref[copy * places + place, :, :width] = piece
-    blocks.put(0)
 
 
 def sum_lat(scale, blocks):
@@ -443,10 +455,9 @@
     arrived = [blocks.get(quad) for quad in range(4)]
     grad_f = take_quads(arrived, hold_ref, 0)
     qkv_ref, probs_ref, w_out_ref = blocks.get(5), blocks.get(6), blocks.get(7)
-    back_attend(
-        grad_f.astype(bf16), qkv_ref, probs_ref, None, w_out_ref, grad_mixed_ref, turned_ref,
-        grad_rows_ref,
-    )
+    for part in range(3):
+        prepare_back(part, grad_f.astype(bf16), qkv_ref, w_out_ref, grad_mixed_ref, turned_ref)
+    back_attend(qkv_ref, probs_ref, None, grad_mixed_ref, turned_ref, grad_rows_ref)
     gain = blocks.get(8)[0:1, :]
     grad_input = back_norm(
         grad_f, normed, inv_std, gain, grad_rows_ref, lambda part: blocks.get(10 + part)
@@ -571,7 +582,7 @@
     partner = lax.ppermute(other, "core", [(i, (i + 1) % n_core) for i in range(n_core)])
     (terms,) = call(
         weight_terms,
-        [(own, HBM, None), (partner, HBM, None)],
+        [(own, pltpu.VMEM, None), (partner, pltpu.VMEM, None)],
         [((n_member * n_pair, rows, D), bf16, HBM)],
         [pltpu.SemaphoreType.DMA((2,))],
         3_000_000_000,
@@ -582,8 +593,8 @@
     parts = lax.all_to_all(terms, ("member", "pair"), 0, 0, tiled=True)
     (plane_sum,) = call(
         sum_plane,
-        [(parts, HBM, None), (after, pl.ANY, None)],
-        [((n_member * n_lat, rows, -(-width // 128) * 128), bf16, HBM)],
+        [(parts, pltpu.VMEM, None), (after, pl.ANY, None)],
+        [((n_member * n_lat, rows, -(-width // 128) * 128), bf16, pltpu.VMEM)],
         [],
         5_000_000,
         "sum_plane",
@@ -592,7 +603,7 @@
     parts = lax.all_to_all(plane_sum, ("member", "lat"), 0, 0, tiled=True)
     (total,) = call(
         functools.partial(sum_lat, scale),
-        [(parts, HBM, None)],
+        [(parts, pltpu.VMEM, None)],
         [((2, rows, width), f32, HBM)],
         [],
         1_000_000,
@@ -665,20 +676,24 @@
             (wide, HBM, None),
             (core.reshape(1), SMEM, None),
         ],
-        [((HEADS, WIN, WIN), f32, HBM), ((2, D // 2, D), bf16, HBM)],
-        gather_scratch + [pltpu.VMEM((WIN, WIN), f32), pltpu.SemaphoreType.DMA((3,))],
+        [
+            ((HEADS, WIN, WIN), f32, pltpu.VMEM),
+            ((2, D // 2, D), bf16, pltpu.VMEM),
+        ],
+        gather_scratch + [pltpu.VMEM((WIN, WIN), f32)],
         5_000_000_000,
         "second_bias",
+        12,
     )
     second = call(
         second_block,
-        [(quad, HBM, None) for quad in shifted]
+        [(quad, pltpu.VMEM, None) for quad in shifted]
         + [
             (norm_gain, HBM, None),
-            *qkv_parts(1),
-            (bias_two, HBM, None),
-            (out_weight, HBM, 1),
-            (picks, HBM, None),
+            (qkv_weight, pltpu.VMEM, None),
+            (out_weight, pltpu.VMEM, None),
+            (bias_two, pltpu.VMEM, None),
+            (picks, pltpu.VMEM, None),
         ],
         [((QUAD, 2 * D), bf16, HBM)] * 4 + [((WIN, 3 * D), bf16, HBM)] * 2,
         [hold, mixed_scratch, pltpu.VMEM((WIN, 3 * D), bf16), pltpu.VMEM((HEADS, WIN, WIN), bf16)]
@@ -686,6 +701,7 @@
         + [pltpu.SemaphoreType.DMA((8,))],
         15_000_000_000,
         "second_block",
+        16,
     )
     returned = exchange(second[:4], False)
     grad_fields, output = call(

time: 92.7 us -> 87 us (0.939)
  Pallas kernels: 42.1 us -> 37.5 us
  blocking collectives: 16 us -> 14.4 us
  waiting for transfers between devices: 15.2 us -> 16.6 us
    pallas_call x7, Pallas kernels: 42.1 us -> 37.5 us  [call(): pl.pallas_call(run, out_shape=[jax.ShapeDtypeStruct(shape, kind) for shap...]
    ppermute x6, waiting for transfers between devices: 3.98 us -> 5.99 us  [moved(): return lax.ppermute(shard, ('lat', 'pair', 'core'), pairs)]
    all_to_all x1, blocking collectives: 16 us -> 14.4 us  [reduce_terms(): parts = lax.all_to_all(plane_sum, ('member', 'lat'), 0, 0, tiled=True)]
    unnamed x16 -> x28, local copies, waits for them, and re-layouts: 2.79 us -> 1.89 us
where the time goes in v2:
time: 87 us; the launch traced here: 86.7 us
  Pallas kernels  37.5 us (43%)
  waiting for transfers between devices  16.6 us (19%)
  starting transfers between devices  15.3 us (18%)
  blocking collectives  14.4 us (17%)
  local copies, waits for them, and re-layouts  1.89 us (2%)
  between operations  1.05 us (1%)
    pallas_call x7, Pallas kernels, call(): pl.pallas_call(run, out_shape=[jax.ShapeDtypeStruct(shape, kind) for shap...  37.5 us
    all_to_all x1, blocking collectives, reduce_terms(): parts = lax.all_to_all(plane_sum, ('member', 'lat'), 0, 0, tiled=True)  14.4 us
    ppermute x6, starting transfers between devices, moved(): return lax.ppermute(shard, ('lat', 'pair', 'core'), pairs)  11.2 us
    all_to_all x1, waiting for transfers between devices, reduce_terms(): parts = lax.all_to_all(terms, ('member', 'pair'), 0, 0, tiled=True)  9.27 us
    ppermute x6, waiting for transfers between devices, moved(): return lax.ppermute(shard, ('lat', 'pair', 'core'), pairs)  5.99 us
    all_to_all x1, starting transfers between devices, reduce_terms(): parts = lax.all_to_all(terms, ('member', 'pair'), 0, 0, tiled=True)  3.71 us
    unnamed x28, local copies, waits for them, and re-layouts  1.89 us
  transfers between devices with their start and end apart: 8, of which 3 were waited for; matrix products, arithmetic and copies ran while one was open for 0% of the time, Pallas kernels for 20%

profile of v2, /device:TPU:32, one launch (start us, length us, event | category | flops | bytes accessed | tf_op | source)
XLA Modules:
  0.0 86.7 jit_solution(11672404748484375748)
XLA Ops:
  0.7 0.0 copy-start.8
  0.7 0.0 copy-start.9
  0.7 9.7 %first_forward.1 = (bf16[36,2304]{1,0:T(8,128)(2,1)}, bf16[36,2304]{1,0:T(8,128)(2,1)}, bf16[36,2304]{1,0:T(8,128)(2,1)}, bf16[36,2304]{1,0:T(8,128)(2,1)}, s32[...) custom-call(bf16[144,144]{1,0:T(8,128)(2,1)} %constant.22.clone.refs_0_, ...), custom_call_target="tpu_custom_call" | custom-call | flops 1000000000 | bytes 4000000 | tf_op jit(solution)/shard_map/first_forward/pallas_call | solution.py:535
  10.4 4.9 %collective-permute-start = (bf16[36,2304]{1,0:T(8,128)(2,1)}, bf16[36,2304]{1,0:T(8,128)(2,1)S(1)}, u32[]{:S(2)}, u32[]{:S(2)}) collective-permute-start(bf16[36,2304]{1,0:T(8,128)(2,1)} %get-tuple-element.23), channel_id=1, source_target_pairs={{0,15},{1,0},{2,1},{3,2},{4,3},{5,4},{6,5},{7,6},{8,7},{9,8},{10,9... | collective-permute-start | bytes 497672 | tf_op jit(solution)/shard_map/ppermute | solution.py:560
  15.3 0.1 collective-permute-start.1
  15.4 5.7 %collective-permute-start.2 = (bf16[36,2304]{1,0:T(8,128)(2,1)}, bf16[36,2304]{1,0:T(8,128)(2,1)S(1)}, u32[]{:S(2)}, u32[]{:S(2)}) collective-permute-start(bf16[36,2304]{1,0:T(8,128)(2,1)} %get-tuple-element.25), channel_id=1, source_target_pairs={{0,127},{1,112},{2,113},{3,114},{4,115},{5,116},{6,117},{7,118},{8... | collective-permute-start | bytes 497672 | tf_op jit(solution)/shard_map/ppermute | solution.py:560
  21.1 0.9 %copy-done.6 = s32[144,256]{1,0:T(8,128)S(1)} copy-done((s32[144,256]{1,0:T(8,128)S(1)}, s32[144,256]{1,0:T(8,128)}, u32[]{:S(2)}) %copy-start.6) | copy-done | bytes 147480
  22.0 5.5 %second_bias.1 = (f32[24,144,144]{2,1,0:T(8,128)S(1)}, bf16[2,384,768]{2,1,0:T(8,128)(2,1)S(1)}) custom-call(s32[6,2,12]{2,1,0:T(2,128)S(1)} %bitcast.24, s32[1]{0:T(128)} %bitcast.8.refs_1_, bf16[144,12]{1,0:T(8,128)(2,1)S(1)} %copy-done.9, bf16[144,12]{1,0:T(8,128)(2,1)S(1)} %copy-done.8, f32[2,24,759]{2,1,0:T(8,128)S(1)} %bitcast.23, ...), custom_call_target="tpu_custom_call" | custom-call | flops 5000000000 | bytes 4000000 | tf_op jit(solution)/shard_map/second_bias/pallas_call | solution.py:535
  27.6 0.0 collective-permute-done.1.refs_2_
  27.7 9.3 %second_block.1 = (bf16[36,1536]{1,0:T(8,128)(2,1)S(1)}, bf16[36,1536]{1,0:T(8,128)(2,1)S(1)}, bf16[36,1536]{1,0:T(8,128)(2,1)S(1)}, bf16[36,1536]{1,0:T(8,128)(...) custom-call(bf16[36,2304]{1,0:T(8,128)(2,1)S(1)} %copy-done.5, ...), custom_call_target="tpu_custom_call" | custom-call | flops 15000000512 | bytes 4000000 | tf_op jit(solution)/shard_map/second_block/pallas_call | solution.py:535
  37.0 0.4 collective-permute-start.6
  37.4 0.0 collective-permute-start.3
  37.4 0.1 collective-permute-start.4
  37.5 0.4 collective-permute-start.5
  37.9 1.3 %collective-permute-done.6.refs_1_ = bf16[144,2304]{1,0:T(8,128)(2,1)S(1)} collective-permute-done((bf16[144,2304]{1,0:T(8,128)(2,1)S(1)}, bf16[144,2304]{1,0:T(8,128)(2,1)S(1)}, u32[]{:S(2)}, u32[]{:S(2)}) %collective-permute-start.6) | collective-permute-done | bytes 663584 | tf_op jit(solution)/shard_map/ppermute | solution.py:582
  39.2 2.4 %weight_terms.1 = bf16[16,48,768]{2,1,0:T(8,128)(2,1)} custom-call(bf16[144,2304]{1,0:T(8,128)(2,1)S(1)} %get-tuple-element.38.refs_0_, bf16[144,2304]{1,0:T(8,128)(2,1)S(1)} %collective-permute-done.6.refs_1_), custom_call_target="tpu_custom_call" | custom-call | flops 3000000000 | bytes 4000000 | tf_op jit(solution)/shard_map/weight_terms/pallas_call | solution.py:535
  41.6 6.0 %collective-permute-done.3.refs_0_ = bf16[36,1536]{1,0:T(8,128)(2,1)S(1)} collective-permute-done((bf16[36,1536]{1,0:T(8,128)(2,1)S(1)}, bf16[36,1536]{1,0:T(8,128)(2,1)S(1)}, u32[]{:S(2)}, u32[]{:S(2)}) %collective-permute-start.3) | collective-permute-done | bytes 110624 | tf_op jit(solution)/shard_map/ppermute | solution.py:560
  47.6 3.7 %all-to-all-start = ((bf16[16,48,768]{2,1,0:T(8,128)(2,1)}), bf16[16,48,768]{2,1,0:T(8,128)(2,1)S(1)}, u32[]{:S(2)}, u32[]{:S(2)}) async-start(bf16[16,48,768]{2,1,0:T(8,128)(2,1)} %weight_terms.1), calls=%async_computation | async-start | bytes 2359296 | tf_op jit(solution)/shard_map/all_to_all | solution.py:593
  51.3 9.6 %first_backward.1 = (bf16[72,2,768]{2,1,0:T(2,128)(2,1)}, bf16[72,2,768]{2,1,0:T(2,128)(2,1)}) custom-call(bf16[36,1536]{1,0:T(8,128)(2,1)} %copy-done.11, bf16[36,1536]{1,0:T(8,128)(2,1)} %copy-done.12, bf16[36,1536]{1,0:T(8,128)(2,1)} %copy-done.13, bf16[36,1536]{1,0:T(8,128)(2,1)} %copy-done.10, bf16[144,768]{1,0:T(8,128)(2,1)} %get-tuple-element.33.refs_4_, ...), custom_call_target="tpu_custom_call" | custom-call | flops 8999999488 | bytes 4000000 | tf_op jit(solution)/shard_map/first_backward/pallas_call | solution.py:535
  60.9 9.3 %all-to-all-done.refs_0_ = bf16[16,48,768]{2,1,0:T(8,128)(2,1)S(1)} async-done(((bf16[16,48,768]{2,1,0:T(8,128)(2,1)}), bf16[16,48,768]{2,1,0:T(8,128)(2,1)S(1)}, u32[]{:S(2)}, u32[]{:S(2)}) %all-to-all-start) | async-done | bytes 1179680 | tf_op jit(solution)/shard_map/all_to_all | solution.py:593
  70.2 0.9 %copy-done.2 = bf16[72,2,768]{2,1,0:T(2,128)(2,1)S(1)} copy-done((bf16[72,2,768]{2,1,0:T(2,128)(2,1)S(1)}, bf16[72,2,768]{2,1,0:T(2,128)(2,1)}, u32[]{:S(2)}) %copy-start.2) | copy-done | bytes 221208
  71.2 0.3 sum_plane.1
  71.4 14.4 %all_to_all.10.refs_0_ = bf16[16,48,128]{2,1,0:T(8,128)(2,1)S(1)} all-to-all(bf16[16,48,128]{2,1,0:T(8,128)(2,1)S(1)} %sum_plane.1), channel_id=1, replica_groups=mesh['member'=2,'lat'=8,'pair'=8,'core'=2] {'member','lat'}, dimensions={0} | all-to-all | bytes 393216 | tf_op jit(solution)/shard_map/all_to_all | solution.py:603
  85.9 0.7 sum_lat.1
  (28 shorter events, 0.1 us)
Async XLA Ops:
  0.6 20.5 %copy-start.3 = (f32[2,1,759,24]{2,3,1,0:T(8,128)S(1)}, f32[2,1,759,24]{2,3,1,0:T(8,128)}, u32[]{:S(2)}) copy-start(f32[2,1,759,24]{2,3,1,0:T(8,128)} %param.18) | copy-start | bytes 437188
  0.6 20.5 %copy-start.7 = (s32[2,6,12]{2,0,1:T(2,128)S(1)}, s32[2,6,12]{2,0,1:T(2,128)}, u32[]{:S(2)}) copy-start(s32[2,6,12]{2,0,1:T(2,128)} %param.20) | copy-start | bytes 1732
  0.7 20.5 %copy-start.8 = (bf16[144,12]{1,0:T(8,128)(2,1)S(1)}, bf16[144,12]{1,0:T(8,128)(2,1)}, u32[]{:S(2)}) copy-start(bf16[144,12]{1,0:T(8,128)(2,1)} %constant.26.clone.refs_3_) | copy-start | bytes 10372
  0.7 20.5 %copy-start.9 = (bf16[144,12]{1,0:T(8,128)(2,1)S(1)}, bf16[144,12]{1,0:T(8,128)(2,1)}, u32[]{:S(2)}) copy-start(bf16[144,12]{1,0:T(8,128)(2,1)} %constant.25.clone.refs_2_) | copy-start | bytes 10372
  10.4 17.2 %collective-permute-start = (bf16[36,2304]{1,0:T(8,128)(2,1)}, bf16[36,2304]{1,0:T(8,128)(2,1)S(1)}, u32[]{:S(2)}, u32[]{:S(2)}) collective-permute-start(bf16[36,2304]{1,0:T(8,128)(2,1)} %get-tuple-element.23), channel_id=1, source_target_pairs={{0,15},{1,0},{2,1},{3,2},{4,3},{5,4},{6,5},{7,6},{8,7},{9,8},{10,9... | collective-permute-start | bytes 497672 | tf_op jit(solution)/shard_map/ppermute | solution.py:560
  15.3 12.3 %collective-permute-start.1 = (bf16[36,2304]{1,0:T(8,128)(2,1)}, bf16[36,2304]{1,0:T(8,128)(2,1)S(1)}, u32[]{:S(2)}, u32[]{:S(2)}) collective-permute-start(bf16[36,2304]{1,0:T(8,128)(2,1)} %get-tuple-element.24), channel_id=1, source_target_pairs={{0,112},{1,113},{2,114},{3,115},{4,116},{5,117},{6,118},{7,119},{8... | collective-permute-start | bytes 497672 | tf_op jit(solution)/shard_map/ppermute | solution.py:560
  15.4 12.2 %collective-permute-start.2 = (bf16[36,2304]{1,0:T(8,128)(2,1)}, bf16[36,2304]{1,0:T(8,128)(2,1)S(1)}, u32[]{:S(2)}, u32[]{:S(2)}) collective-permute-start(bf16[36,2304]{1,0:T(8,128)(2,1)} %get-tuple-element.25), channel_id=1, source_target_pairs={{0,127},{1,112},{2,113},{3,114},{4,115},{5,116},{6,117},{7,118},{8... | collective-permute-start | bytes 497672 | tf_op jit(solution)/shard_map/ppermute | solution.py:560
  21.1 0.9 %copy-start.6 = (s32[144,256]{1,0:T(8,128)S(1)}, s32[144,256]{1,0:T(8,128)}, u32[]{:S(2)}) copy-start(s32[144,256]{1,0:T(8,128)} %get-tuple-element.26.refs_5_) | copy-start | bytes 442372
  22.0 5.6 %copy-start = (bf16[2,768,2304]{2,1,0:T(8,128)(2,1)S(1)}, bf16[2,768,2304]{2,1,0:T(8,128)(2,1)}, u32[]{:S(2)}) copy-start(bf16[2,768,2304]{2,1,0:T(8,128)(2,1)} %refs_12_.1) | copy-start | bytes 21233668
  22.0 5.6 %copy-start.1 = (bf16[2,768,768]{2,1,0:T(8,128)(2,1)S(1)}, bf16[2,768,768]{2,1,0:T(8,128)(2,1)}, u32[]{:S(2)}) copy-start(bf16[2,768,768]{2,1,0:T(8,128)(2,1)} %refs_7_.3) | copy-start | bytes 7077892
  22.0 5.6 %copy-start.4 = (f32[2,768]{1,0:T(2,128)S(1)}, f32[2,768]{1,0:T(2,128)}, u32[]{:S(2)}) copy-start(f32[2,768]{1,0:T(2,128)} %refs_8_.3) | copy-start | bytes 18436
  22.0 5.6 %copy-start.5 = (bf16[36,2304]{1,0:T(8,128)(2,1)S(1)}, bf16[36,2304]{1,0:T(8,128)(2,1)}, u32[]{:S(2)}) copy-start(bf16[36,2304]{1,0:T(8,128)(2,1)} %get-tuple-element.22.refs_0_) | copy-start | bytes 497668
  37.0 4.6 %copy-start.10 = (bf16[36,1536]{1,0:T(8,128)(2,1)}, bf16[36,1536]{1,0:T(8,128)(2,1)S(1)}, u32[]{:S(2)}) copy-start(bf16[36,1536]{1,0:T(8,128)(2,1)S(1)} %get-tuple-element.32.refs_3_) | copy-start | bytes 331780
  37.0 2.2 %collective-permute-start.6 = (bf16[144,2304]{1,0:T(8,128)(2,1)S(1)}, bf16[144,2304]{1,0:T(8,128)(2,1)S(1)}, u32[]{:S(2)}, u32[]{:S(2)}) collective-permute-start(bf16[144,2304]{1,0:T(8,128)(2,1)S(1)} %get-tuple-element.39), channel_id=1, source_target_pairs={{0,1},{1,0},{2,3},{3,2},{4,5},{5,4},{6,7},{7,6},{8,9},{9,8},{10,11... | collective-permute-start | bytes 1990664 | tf_op jit(solution)/shard_map/ppermute | solution.py:582
  37.4 10.2 %collective-permute-start.3 = (bf16[36,1536]{1,0:T(8,128)(2,1)S(1)}, bf16[36,1536]{1,0:T(8,128)(2,1)S(1)}, u32[]{:S(2)}, u32[]{:S(2)}) collective-permute-start(bf16[36,1536]{1,0:T(8,128)(2,1)S(1)} %get-tuple-element.29), channel_id=1, source_target_pairs={{0,17},{1,18},{2,19},{3,20},{4,21},{5,22},{6,23},{7,24},{8,25},{9,... | collective-permute-start | bytes 331784 | tf_op jit(solution)/shard_map/ppermute | solution.py:560
  37.4 10.1 %collective-permute-start.4 = (bf16[36,1536]{1,0:T(8,128)(2,1)S(1)}, bf16[36,1536]{1,0:T(8,128)(2,1)S(1)}, u32[]{:S(2)}, u32[]{:S(2)}) collective-permute-start(bf16[36,1536]{1,0:T(8,128)(2,1)S(1)} %get-tuple-element.30), channel_id=1, source_target_pairs={{0,16},{1,17},{2,18},{3,19},{4,20},{5,21},{6,22},{7,23},{8,24},{9,... | collective-permute-start | bytes 331784 | tf_op jit(solution)/shard_map/ppermute | solution.py:560
  37.5 10.1 %collective-permute-start.5 = (bf16[36,1536]{1,0:T(8,128)(2,1)S(1)}, bf16[36,1536]{1,0:T(8,128)(2,1)S(1)}, u32[]{:S(2)}, u32[]{:S(2)}) collective-permute-start(bf16[36,1536]{1,0:T(8,128)(2,1)S(1)} %get-tuple-element.31), channel_id=1, source_target_pairs={{0,1},{1,2},{2,3},{3,4},{4,5},{5,6},{6,7},{7,8},{8,9},{9,10},{10,1... | collective-permute-start | bytes 331784 | tf_op jit(solution)/shard_map/ppermute | solution.py:560
  47.6 3.7 %copy-start.11 = (bf16[36,1536]{1,0:T(8,128)(2,1)}, bf16[36,1536]{1,0:T(8,128)(2,1)S(1)}, u32[]{:S(2)}) copy-start(bf16[36,1536]{1,0:T(8,128)(2,1)S(1)} %collective-permute-done.3.refs_0_) | copy-start | bytes 331780
  47.6 3.7 %copy-start.12 = (bf16[36,1536]{1,0:T(8,128)(2,1)}, bf16[36,1536]{1,0:T(8,128)(2,1)S(1)}, u32[]{:S(2)}) copy-start(bf16[36,1536]{1,0:T(8,128)(2,1)S(1)} %collective-permute-done.4.refs_1_) | copy-start | bytes 331780
  47.6 3.8 %copy-start.13 = (bf16[36,1536]{1,0:T(8,128)(2,1)}, bf16[36,1536]{1,0:T(8,128)(2,1)S(1)}, u32[]{:S(2)}) copy-start(bf16[36,1536]{1,0:T(8,128)(2,1)S(1)} %collective-permute-done.5.refs_2_) | copy-start | bytes 331780
  47.6 22.6 %all-to-all-start = ((bf16[16,48,768]{2,1,0:T(8,128)(2,1)}), bf16[16,48,768]{2,1,0:T(8,128)(2,1)S(1)}, u32[]{:S(2)}, u32[]{:S(2)}) async-start(bf16[16,48,768]{2,1,0:T(8,128)(2,1)} %weight_terms.1), calls=%async_computation | async-start | bytes 2359296 | tf_op jit(solution)/shard_map/all_to_all | solution.py:593
  70.2 0.9 %copy-start.2 = (bf16[72,2,768]{2,1,0:T(2,128)(2,1)S(1)}, bf16[72,2,768]{2,1,0:T(2,128)(2,1)}, u32[]{:S(2)}) copy-start(bf16[72,2,768]{2,1,0:T(2,128)(2,1)} %get-tuple-element.37.refs_1_) | copy-start | bytes 663556

commit v3 on v2

--- a/solution.py
+++ b/solution.py
@@ -409,13 +409,17 @@
     n_parts, rows, _ = terms_ref.shape
     n_parts //= 2
     half = n_parts * rows
-    unit = eye(half)
+    unit = eye(128)
     packs = (blocks.get(0), blocks.get(1))
     for block in range(2):
         cols = slice(2 * D + block * half, 2 * D + (block + 1) * half)
         total = jnp.zeros((half, D), f32)
         for pack in packs:
-            turned = mm_t(unit, pack[:, cols]).astype(bf16)
+            turned = [
+                mm_t(unit, pack[:, start : start + 128]).astype(bf16)
+                for start in range(cols.start, cols.stop, 128)
+            ]
+            turned = jnp.concatenate(turned, axis=0)
             total += mm(turned, pack[:, block * D : (block + 1) * D])
         for part in range(n_parts):
             piece = total[part * rows : (part + 1) * rows, :].astype(bf16)
@@ -560,12 +564,9 @@
         return lax.ppermute(shard, ("lat", "pair", "core"), pairs)
 
     if forward:
-        return (
-            quads[3],
-            moved(quads[2], 0, 1),
-            moved(quads[1], 1, 0),
-            moved(quads[0], 1, 1),
-        )
+        corner = moved(quads[0], 1, 1)
+        row = moved(quads[1], 1, 0)
+        return quads[3], moved(quads[2], 0, 1), row, corner
     return (
         moved(quads[3], 1, 1),
         moved(quads[2], 1, 0),

time: 87 us -> 87 us (level)
  no operation moved by 1% of the time
where the time goes in v3:
time: 87 us; the launch traced here: 86.7 us
  Pallas kernels  37.1 us (43%)
  waiting for transfers between devices  16.9 us (19%)
  starting transfers between devices  15.3 us (18%)
  blocking collectives  14.4 us (17%)
  local copies, waits for them, and re-layouts  1.89 us (2%)
  between operations  1.05 us (1%)
    pallas_call x7, Pallas kernels, call(): pl.pallas_call(run, out_shape=[jax.ShapeDtypeStruct(shape, kind) for shap...  37.1 us
    all_to_all x1, blocking collectives, reduce_terms(): parts = lax.all_to_all(plane_sum, ('member', 'lat'), 0, 0, tiled=True)  14.4 us
    ppermute x6, starting transfers between devices, moved(): return lax.ppermute(shard, ('lat', 'pair', 'core'), pairs)  11.2 us
    all_to_all x1, waiting for transfers between devices, reduce_terms(): parts = lax.all_to_all(terms, ('member', 'pair'), 0, 0, tiled=True)  9.27 us
    ppermute x6, waiting for transfers between devices, moved(): return lax.ppermute(shard, ('lat', 'pair', 'core'), pairs)  6.36 us
    all_to_all x1, starting transfers between devices, reduce_terms(): parts = lax.all_to_all(terms, ('member', 'pair'), 0, 0, tiled=True)  3.71 us
    unnamed x28, local copies, waits for them, and re-layouts  1.89 us
  transfers between devices with their start and end apart: 8, of which 3 were waited for; matrix products, arithmetic and copies ran while one was open for 0% of the time, Pallas kernels for 20%

profile of v3, /device:TPU:32, one launch (start us, length us, event | category | flops | bytes accessed | tf_op | source)
XLA Modules:
  0.0 86.7 jit_solution(10533072672832332288)
XLA Ops:
  0.7 0.0 copy-start.8
  0.7 0.0 copy-start.9
  0.7 9.7 %first_forward.1 = (bf16[36,2304]{1,0:T(8,128)(2,1)}, bf16[36,2304]{1,0:T(8,128)(2,1)}, bf16[36,2304]{1,0:T(8,128)(2,1)}, bf16[36,2304]{1,0:T(8,128)(2,1)}, s32[...) custom-call(bf16[144,144]{1,0:T(8,128)(2,1)} %constant.22.clone.refs_0_, ...), custom_call_target="tpu_custom_call" | custom-call | flops 1000000000 | bytes 4000000 | tf_op jit(solution)/shard_map/first_forward/pallas_call | solution.py:539
  10.4 4.9 %collective-permute-start = (bf16[36,2304]{1,0:T(8,128)(2,1)}, bf16[36,2304]{1,0:T(8,128)(2,1)S(1)}, u32[]{:S(2)}, u32[]{:S(2)}) collective-permute-start(bf16[36,2304]{1,0:T(8,128)(2,1)} %get-tuple-element.23), channel_id=1, source_target_pairs={{0,15},{1,0},{2,1},{3,2},{4,3},{5,4},{6,5},{7,6},{8,7},{9,8},{10,9... | collective-permute-start | bytes 497672 | tf_op jit(solution)/shard_map/ppermute | solution.py:564
  15.3 0.1 collective-permute-start.1
  15.4 5.7 %collective-permute-start.2 = (bf16[36,2304]{1,0:T(8,128)(2,1)}, bf16[36,2304]{1,0:T(8,128)(2,1)S(1)}, u32[]{:S(2)}, u32[]{:S(2)}) collective-permute-start(bf16[36,2304]{1,0:T(8,128)(2,1)} %get-tuple-element.25), channel_id=1, source_target_pairs={{0,127},{1,112},{2,113},{3,114},{4,115},{5,116},{6,117},{7,118},{8... | collective-permute-start | bytes 497672 | tf_op jit(solution)/shard_map/ppermute | solution.py:564
  21.1 0.9 %copy-done.6 = s32[144,256]{1,0:T(8,128)S(1)} copy-done((s32[144,256]{1,0:T(8,128)S(1)}, s32[144,256]{1,0:T(8,128)}, u32[]{:S(2)}) %copy-start.6) | copy-done | bytes 147480
  22.0 5.5 %second_bias.1 = (f32[24,144,144]{2,1,0:T(8,128)S(1)}, bf16[2,384,768]{2,1,0:T(8,128)(2,1)S(1)}) custom-call(s32[6,2,12]{2,1,0:T(2,128)S(1)} %bitcast.24, s32[1]{0:T(128)} %bitcast.8.refs_1_, bf16[144,12]{1,0:T(8,128)(2,1)S(1)} %copy-done.9, bf16[144,12]{1,0:T(8,128)(2,1)S(1)} %copy-done.8, f32[2,24,759]{2,1,0:T(8,128)S(1)} %bitcast.23, ...), custom_call_target="tpu_custom_call" | custom-call | flops 5000000000 | bytes 4000000 | tf_op jit(solution)/shard_map/second_bias/pallas_call | solution.py:539
  27.6 0.0 collective-permute-done.1.refs_2_
  27.7 9.3 %second_block.1 = (bf16[36,1536]{1,0:T(8,128)(2,1)S(1)}, bf16[36,1536]{1,0:T(8,128)(2,1)S(1)}, bf16[36,1536]{1,0:T(8,128)(2,1)S(1)}, bf16[36,1536]{1,0:T(8,128)(...) custom-call(bf16[36,2304]{1,0:T(8,128)(2,1)S(1)} %copy-done.5, ...), custom_call_target="tpu_custom_call" | custom-call | flops 15000000512 | bytes 4000000 | tf_op jit(solution)/shard_map/second_block/pallas_call | solution.py:539
  37.0 0.4 collective-permute-start.6
  37.4 0.0 collective-permute-start.3
  37.4 0.1 collective-permute-start.4
  37.5 0.4 collective-permute-start.5
  37.9 1.3 %collective-permute-done.6.refs_1_ = bf16[144,2304]{1,0:T(8,128)(2,1)S(1)} collective-permute-done((bf16[144,2304]{1,0:T(8,128)(2,1)S(1)}, bf16[144,2304]{1,0:T(8,128)(2,1)S(1)}, u32[]{:S(2)}, u32[]{:S(2)}) %collective-permute-start.6) | collective-permute-done | bytes 663584 | tf_op jit(solution)/shard_map/ppermute | solution.py:583
  39.2 2.0 %weight_terms.1 = bf16[16,48,768]{2,1,0:T(8,128)(2,1)} custom-call(bf16[144,2304]{1,0:T(8,128)(2,1)S(1)} %get-tuple-element.38.refs_0_, bf16[144,2304]{1,0:T(8,128)(2,1)S(1)} %collective-permute-done.6.refs_1_), custom_call_target="tpu_custom_call" | custom-call | flops 3000000000 | bytes 4000000 | tf_op jit(solution)/shard_map/weight_terms/pallas_call | solution.py:539
  41.2 6.3 %collective-permute-done.3.refs_0_ = bf16[36,1536]{1,0:T(8,128)(2,1)S(1)} collective-permute-done((bf16[36,1536]{1,0:T(8,128)(2,1)S(1)}, bf16[36,1536]{1,0:T(8,128)(2,1)S(1)}, u32[]{:S(2)}, u32[]{:S(2)}) %collective-permute-start.3) | collective-permute-done | bytes 110624 | tf_op jit(solution)/shard_map/ppermute | solution.py:564
  47.6 3.7 %all-to-all-start = ((bf16[16,48,768]{2,1,0:T(8,128)(2,1)}), bf16[16,48,768]{2,1,0:T(8,128)(2,1)S(1)}, u32[]{:S(2)}, u32[]{:S(2)}) async-start(bf16[16,48,768]{2,1,0:T(8,128)(2,1)} %weight_terms.1), calls=%async_computation | async-start | bytes 2359296 | tf_op jit(solution)/shard_map/all_to_all | solution.py:594
  51.3 9.6 %first_backward.1 = (bf16[72,2,768]{2,1,0:T(2,128)(2,1)}, bf16[72,2,768]{2,1,0:T(2,128)(2,1)}) custom-call(bf16[36,1536]{1,0:T(8,128)(2,1)} %copy-done.11, bf16[36,1536]{1,0:T(8,128)(2,1)} %copy-done.12, bf16[36,1536]{1,0:T(8,128)(2,1)} %copy-done.13, bf16[36,1536]{1,0:T(8,128)(2,1)} %copy-done.10, bf16[144,768]{1,0:T(8,128)(2,1)} %get-tuple-element.33.refs_4_, ...), custom_call_target="tpu_custom_call" | custom-call | flops 8999999488 | bytes 4000000 | tf_op jit(solution)/shard_map/first_backward/pallas_call | solution.py:539
  60.9 9.3 %all-to-all-done.refs_0_ = bf16[16,48,768]{2,1,0:T(8,128)(2,1)S(1)} async-done(((bf16[16,48,768]{2,1,0:T(8,128)(2,1)}), bf16[16,48,768]{2,1,0:T(8,128)(2,1)S(1)}, u32[]{:S(2)}, u32[]{:S(2)}) %all-to-all-start) | async-done | bytes 1179680 | tf_op jit(solution)/shard_map/all_to_all | solution.py:594
  70.2 0.9 %copy-done.2 = bf16[72,2,768]{2,1,0:T(2,128)(2,1)S(1)} copy-done((bf16[72,2,768]{2,1,0:T(2,128)(2,1)S(1)}, bf16[72,2,768]{2,1,0:T(2,128)(2,1)}, u32[]{:S(2)}) %copy-start.2) | copy-done | bytes 221208
  71.2 0.3 sum_plane.1
  71.4 14.4 %all_to_all.10.refs_0_ = bf16[16,48,128]{2,1,0:T(8,128)(2,1)S(1)} all-to-all(bf16[16,48,128]{2,1,0:T(8,128)(2,1)S(1)} %sum_plane.1), channel_id=1, replica_groups=mesh['member'=2,'lat'=8,'pair'=8,'core'=2] {'member','lat'}, dimensions={0} | all-to-all | bytes 393216 | tf_op jit(solution)/shard_map/all_to_all | solution.py:604
  85.9 0.7 sum_lat.1
  (28 shorter events, 0.1 us)
Async XLA Ops:
  0.6 20.5 %copy-start.3 = (f32[2,1,759,24]{2,3,1,0:T(8,128)S(1)}, f32[2,1,759,24]{2,3,1,0:T(8,128)}, u32[]{:S(2)}) copy-start(f32[2,1,759,24]{2,3,1,0:T(8,128)} %param.18) | copy-start | bytes 437188
  0.6 20.5 %copy-start.7 = (s32[2,6,12]{2,0,1:T(2,128)S(1)}, s32[2,6,12]{2,0,1:T(2,128)}, u32[]{:S(2)}) copy-start(s32[2,6,12]{2,0,1:T(2,128)} %param.20) | copy-start | bytes 1732
  0.7 20.5 %copy-start.8 = (bf16[144,12]{1,0:T(8,128)(2,1)S(1)}, bf16[144,12]{1,0:T(8,128)(2,1)}, u32[]{:S(2)}) copy-start(bf16[144,12]{1,0:T(8,128)(2,1)} %constant.26.clone.refs_3_) | copy-start | bytes 10372
  0.7 20.5 %copy-start.9 = (bf16[144,12]{1,0:T(8,128)(2,1)S(1)}, bf16[144,12]{1,0:T(8,128)(2,1)}, u32[]{:S(2)}) copy-start(bf16[144,12]{1,0:T(8,128)(2,1)} %constant.25.clone.refs_2_) | copy-start | bytes 10372
  10.4 17.2 %collective-permute-start = (bf16[36,2304]{1,0:T(8,128)(2,1)}, bf16[36,2304]{1,0:T(8,128)(2,1)S(1)}, u32[]{:S(2)}, u32[]{:S(2)}) collective-permute-start(bf16[36,2304]{1,0:T(8,128)(2,1)} %get-tuple-element.23), channel_id=1, source_target_pairs={{0,15},{1,0},{2,1},{3,2},{4,3},{5,4},{6,5},{7,6},{8,7},{9,8},{10,9... | collective-permute-start | bytes 497672 | tf_op jit(solution)/shard_map/ppermute | solution.py:564
  15.3 12.3 %collective-permute-start.1 = (bf16[36,2304]{1,0:T(8,128)(2,1)}, bf16[36,2304]{1,0:T(8,128)(2,1)S(1)}, u32[]{:S(2)}, u32[]{:S(2)}) collective-permute-start(bf16[36,2304]{1,0:T(8,128)(2,1)} %get-tuple-element.24), channel_id=1, source_target_pairs={{0,112},{1,113},{2,114},{3,115},{4,116},{5,117},{6,118},{7,119},{8... | collective-permute-start | bytes 497672 | tf_op jit(solution)/shard_map/ppermute | solution.py:564
  15.4 12.2 %collective-permute-start.2 = (bf16[36,2304]{1,0:T(8,128)(2,1)}, bf16[36,2304]{1,0:T(8,128)(2,1)S(1)}, u32[]{:S(2)}, u32[]{:S(2)}) collective-permute-start(bf16[36,2304]{1,0:T(8,128)(2,1)} %get-tuple-element.25), channel_id=1, source_target_pairs={{0,127},{1,112},{2,113},{3,114},{4,115},{5,116},{6,117},{7,118},{8... | collective-permute-start | bytes 497672 | tf_op jit(solution)/shard_map/ppermute | solution.py:564
  21.1 0.9 %copy-start.6 = (s32[144,256]{1,0:T(8,128)S(1)}, s32[144,256]{1,0:T(8,128)}, u32[]{:S(2)}) copy-start(s32[144,256]{1,0:T(8,128)} %get-tuple-element.26.refs_5_) | copy-start | bytes 442372
  22.0 5.6 %copy-start = (bf16[2,768,2304]{2,1,0:T(8,128)(2,1)S(1)}, bf16[2,768,2304]{2,1,0:T(8,128)(2,1)}, u32[]{:S(2)}) copy-start(bf16[2,768,2304]{2,1,0:T(8,128)(2,1)} %refs_12_.1) | copy-start | bytes 21233668
  22.0 5.6 %copy-start.1 = (bf16[2,768,768]{2,1,0:T(8,128)(2,1)S(1)}, bf16[2,768,768]{2,1,0:T(8,128)(2,1)}, u32[]{:S(2)}) copy-start(bf16[2,768,768]{2,1,0:T(8,128)(2,1)} %refs_7_.3) | copy-start | bytes 7077892
  22.0 5.6 %copy-start.4 = (f32[2,768]{1,0:T(2,128)S(1)}, f32[2,768]{1,0:T(2,128)}, u32[]{:S(2)}) copy-start(f32[2,768]{1,0:T(2,128)} %refs_8_.3) | copy-start | bytes 18436
  22.0 5.6 %copy-start.5 = (bf16[36,2304]{1,0:T(8,128)(2,1)S(1)}, bf16[36,2304]{1,0:T(8,128)(2,1)}, u32[]{:S(2)}) copy-start(bf16[36,2304]{1,0:T(8,128)(2,1)} %get-tuple-element.22.refs_0_) | copy-start | bytes 497668
  37.0 4.2 %copy-start.10 = (bf16[36,1536]{1,0:T(8,128)(2,1)}, bf16[36,1536]{1,0:T(8,128)(2,1)S(1)}, u32[]{:S(2)}) copy-start(bf16[36,1536]{1,0:T(8,128)(2,1)S(1)} %get-tuple-element.32.refs_3_) | copy-start | bytes 331780
  37.0 2.2 %collective-permute-start.6 = (bf16[144,2304]{1,0:T(8,128)(2,1)S(1)}, bf16[144,2304]{1,0:T(8,128)(2,1)S(1)}, u32[]{:S(2)}, u32[]{:S(2)}) collective-permute-start(bf16[144,2304]{1,0:T(8,128)(2,1)S(1)} %get-tuple-element.39), channel_id=1, source_target_pairs={{0,1},{1,0},{2,3},{3,2},{4,5},{5,4},{6,7},{7,6},{8,9},{9,8},{10,11... | collective-permute-start | bytes 1990664 | tf_op jit(solution)/shard_map/ppermute | solution.py:583
  37.4 10.2 %collective-permute-start.3 = (bf16[36,1536]{1,0:T(8,128)(2,1)S(1)}, bf16[36,1536]{1,0:T(8,128)(2,1)S(1)}, u32[]{:S(2)}, u32[]{:S(2)}) collective-permute-start(bf16[36,1536]{1,0:T(8,128)(2,1)S(1)} %get-tuple-element.29), channel_id=1, source_target_pairs={{0,17},{1,18},{2,19},{3,20},{4,21},{5,22},{6,23},{7,24},{8,25},{9,... | collective-permute-start | bytes 331784 | tf_op jit(solution)/shard_map/ppermute | solution.py:564
  37.4 10.1 %collective-permute-start.4 = (bf16[36,1536]{1,0:T(8,128)(2,1)S(1)}, bf16[36,1536]{1,0:T(8,128)(2,1)S(1)}, u32[]{:S(2)}, u32[]{:S(2)}) collective-permute-start(bf16[36,1536]{1,0:T(8,128)(2,1)S(1)} %get-tuple-element.30), channel_id=1, source_target_pairs={{0,16},{1,17},{2,18},{3,19},{4,20},{5,21},{6,22},{7,23},{8,24},{9,... | collective-permute-start | bytes 331784 | tf_op jit(solution)/shard_map/ppermute | solution.py:564
  37.5 10.1 %collective-permute-start.5 = (bf16[36,1536]{1,0:T(8,128)(2,1)S(1)}, bf16[36,1536]{1,0:T(8,128)(2,1)S(1)}, u32[]{:S(2)}, u32[]{:S(2)}) collective-permute-start(bf16[36,1536]{1,0:T(8,128)(2,1)S(1)} %get-tuple-element.31), channel_id=1, source_target_pairs={{0,1},{1,2},{2,3},{3,4},{4,5},{5,6},{6,7},{7,8},{8,9},{9,10},{10,1... | collective-permute-start | bytes 331784 | tf_op jit(solution)/shard_map/ppermute | solution.py:564
  47.6 3.7 %copy-start.11 = (bf16[36,1536]{1,0:T(8,128)(2,1)}, bf16[36,1536]{1,0:T(8,128)(2,1)S(1)}, u32[]{:S(2)}) copy-start(bf16[36,1536]{1,0:T(8,128)(2,1)S(1)} %collective-permute-done.3.refs_0_) | copy-start | bytes 331780
  47.6 3.7 %copy-start.12 = (bf16[36,1536]{1,0:T(8,128)(2,1)}, bf16[36,1536]{1,0:T(8,128)(2,1)S(1)}, u32[]{:S(2)}) copy-start(bf16[36,1536]{1,0:T(8,128)(2,1)S(1)} %collective-permute-done.4.refs_1_) | copy-start | bytes 331780
  47.6 3.8 %copy-start.13 = (bf16[36,1536]{1,0:T(8,128)(2,1)}, bf16[36,1536]{1,0:T(8,128)(2,1)S(1)}, u32[]{:S(2)}) copy-start(bf16[36,1536]{1,0:T(8,128)(2,1)S(1)} %collective-permute-done.5.refs_2_) | copy-start | bytes 331780
  47.6 22.6 %all-to-all-start = ((bf16[16,48,768]{2,1,0:T(8,128)(2,1)}), bf16[16,48,768]{2,1,0:T(8,128)(2,1)S(1)}, u32[]{:S(2)}, u32[]{:S(2)}) async-start(bf16[16,48,768]{2,1,0:T(8,128)(2,1)} %weight_terms.1), calls=%async_computation | async-start | bytes 2359296 | tf_op jit(solution)/shard_map/all_to_all | solution.py:594
  70.2 0.9 %copy-start.2 = (bf16[72,2,768]{2,1,0:T(2,128)(2,1)S(1)}, bf16[72,2,768]{2,1,0:T(2,128)(2,1)}, u32[]{:S(2)}) copy-start(bf16[72,2,768]{2,1,0:T(2,128)(2,1)} %get-tuple-element.37.refs_1_) | copy-start | bytes 663556

commit v4 on v3

--- a/solution.py
+++ b/solution.py
@@ -1,4 +1,5 @@
 import functools
+import math
 
 import jax
 import jax.numpy as jnp
@@ -427,6 +428,10 @@
         blocks.put(0, pl.ds(block * n_parts, n_parts), sems.at[block])
 
 
+def fold(width):
+    return 128 // math.gcd(width, 128)
+
+
 def sum_plane(blocks):
     parts_ref, out_ref = blocks.get(0), blocks.outs[0]
     total = parts_ref[0].astype(f32)
@@ -436,9 +441,15 @@
     places = out_ref.shape[0] // copies
     width = D // places
     for place in range(places):
-        piece = total[:, place * width : (place + 1) * width].astype(bf16)
+        piece = total[:, place * width : (place + 1) * width]
+        folds = fold(width)
+        lines = total.shape[0] // folds
+        flat = [piece[line * lines : (line + 1) * lines] for line in range(folds)]
+        flat = jnp.concatenate(flat, axis=1)
+        tiles = [flat[:, start : start + 128] for start in range(0, folds * width, 128)]
+        piece = jnp.concatenate(tiles, axis=0).astype(bf16)
         for copy in range(copies):
-            out_ref[copy * places + place, :, :width] = piece
+            out_ref[copy * places + place] = piece
 
 
 def sum_lat(scale, blocks):
@@ -449,7 +460,12 @@
         total = parts_ref[block * count].astype(f32)
         for part in range(1, count):
             total += parts_ref[block * count + part].astype(f32)
-        out_ref[block] = total[:, :width] * scale
+        folds = fold(width)
+        lines = out_ref.shape[1] // folds
+        flat = [total[start : start + lines] for start in range(0, total.shape[0], lines)]
+        flat = jnp.concatenate(flat, axis=1) * scale
+        pieces = [flat[:, line * width : (line + 1) * width] for line in range(folds)]
+        out_ref[block] = jnp.concatenate(pieces, axis=0)
     blocks.put(0)
 
 
@@ -595,7 +611,7 @@
     (plane_sum,) = call(
         sum_plane,
         [(parts, pltpu.VMEM, None), (after, pl.ANY, None)],
-        [((n_member * n_lat, rows, -(-width // 128) * 128), bf16, pltpu.VMEM)],
+        [((n_member * n_lat, rows * width // 128, 128), bf16, pltpu.VMEM)],
         [],
         5_000_000,
         "sum_plane",

time: 87 us -> 86.8 us (level)
  no operation moved by 1% of the time
where the time goes in v4:
time: 86.8 us; the launch traced here: 86.6 us
  Pallas kernels  37.2 us (43%)
  waiting for transfers between devices  16.9 us (19%)
  starting transfers between devices  15.3 us (18%)
  blocking collectives  14.2 us (16%)
  local copies, waits for them, and re-layouts  1.89 us (2%)
  between operations  1.05 us (1%)
    pallas_call x7, Pallas kernels, call(): pl.pallas_call(run, out_shape=[jax.ShapeDtypeStruct(shape, kind) for shap...  37.2 us
    all_to_all x1, blocking collectives, reduce_terms(): parts = lax.all_to_all(plane_sum, ('member', 'lat'), 0, 0, tiled=True)  14.2 us
    ppermute x6, starting transfers between devices, moved(): return lax.ppermute(shard, ('lat', 'pair', 'core'), pairs)  11.2 us
    all_to_all x1, waiting for transfers between devices, reduce_terms(): parts = lax.all_to_all(terms, ('member', 'pair'), 0, 0, tiled=True)  9.27 us
    ppermute x6, waiting for transfers between devices, moved(): return lax.ppermute(shard, ('lat', 'pair', 'core'), pairs)  6.36 us
    all_to_all x1, starting transfers between devices, reduce_terms(): parts = lax.all_to_all(terms, ('member', 'pair'), 0, 0, tiled=True)  3.71 us
    unnamed x28, local copies, waits for them, and re-layouts  1.89 us
  transfers between devices with their start and end apart: 8, of which 3 were waited for; matrix products, arithmetic and copies ran while one was open for 0% of the time, Pallas kernels for 20%

profile of v4, /device:TPU:32, one launch (start us, length us, event | category | flops | bytes accessed | tf_op | source)
XLA Modules:
  0.0 86.6 jit_solution(11708876899782923257)
XLA Ops:
  0.7 0.0 copy-start.8
  0.7 0.0 copy-start.9
  0.7 9.7 %first_forward.1 = (bf16[36,2304]{1,0:T(8,128)(2,1)}, bf16[36,2304]{1,0:T(8,128)(2,1)}, bf16[36,2304]{1,0:T(8,128)(2,1)}, bf16[36,2304]{1,0:T(8,128)(2,1)}, s32[...) custom-call(bf16[144,144]{1,0:T(8,128)(2,1)} %constant.22.clone.refs_0_, ...), custom_call_target="tpu_custom_call" | custom-call | flops 1000000000 | bytes 4000000 | tf_op jit(solution)/shard_map/first_forward/pallas_call | solution.py:555
  10.4 4.9 %collective-permute-start = (bf16[36,2304]{1,0:T(8,128)(2,1)}, bf16[36,2304]{1,0:T(8,128)(2,1)S(1)}, u32[]{:S(2)}, u32[]{:S(2)}) collective-permute-start(bf16[36,2304]{1,0:T(8,128)(2,1)} %get-tuple-element.23), channel_id=1, source_target_pairs={{0,15},{1,0},{2,1},{3,2},{4,3},{5,4},{6,5},{7,6},{8,7},{9,8},{10,9... | collective-permute-start | bytes 497672 | tf_op jit(solution)/shard_map/ppermute | solution.py:580
  15.3 0.1 collective-permute-start.1
  15.4 5.7 %collective-permute-start.2 = (bf16[36,2304]{1,0:T(8,128)(2,1)}, bf16[36,2304]{1,0:T(8,128)(2,1)S(1)}, u32[]{:S(2)}, u32[]{:S(2)}) collective-permute-start(bf16[36,2304]{1,0:T(8,128)(2,1)} %get-tuple-element.25), channel_id=1, source_target_pairs={{0,127},{1,112},{2,113},{3,114},{4,115},{5,116},{6,117},{7,118},{8... | collective-permute-start | bytes 497672 | tf_op jit(solution)/shard_map/ppermute | solution.py:580
  21.1 0.9 %copy-done.6 = s32[144,256]{1,0:T(8,128)S(1)} copy-done((s32[144,256]{1,0:T(8,128)S(1)}, s32[144,256]{1,0:T(8,128)}, u32[]{:S(2)}) %copy-start.6) | copy-done | bytes 147480
  22.0 5.5 %second_bias.1 = (f32[24,144,144]{2,1,0:T(8,128)S(1)}, bf16[2,384,768]{2,1,0:T(8,128)(2,1)S(1)}) custom-call(s32[6,2,12]{2,1,0:T(2,128)S(1)} %bitcast.24, s32[1]{0:T(128)} %bitcast.8.refs_1_, bf16[144,12]{1,0:T(8,128)(2,1)S(1)} %copy-done.9, bf16[144,12]{1,0:T(8,128)(2,1)S(1)} %copy-done.8, f32[2,24,759]{2,1,0:T(8,128)S(1)} %bitcast.23, ...), custom_call_target="tpu_custom_call" | custom-call | flops 5000000000 | bytes 4000000 | tf_op jit(solution)/shard_map/second_bias/pallas_call | solution.py:555
  27.6 0.0 collective-permute-done.2.refs_3_
  27.7 9.3 %second_block.1 = (bf16[36,1536]{1,0:T(8,128)(2,1)S(1)}, bf16[36,1536]{1,0:T(8,128)(2,1)S(1)}, bf16[36,1536]{1,0:T(8,128)(2,1)S(1)}, bf16[36,1536]{1,0:T(8,128)(...) custom-call(bf16[36,2304]{1,0:T(8,128)(2,1)S(1)} %copy-done.5, ...), custom_call_target="tpu_custom_call" | custom-call | flops 15000000512 | bytes 4000000 | tf_op jit(solution)/shard_map/second_block/pallas_call | solution.py:555
  37.0 0.4 collective-permute-start.6
  37.4 0.0 collective-permute-start.3
  37.4 0.1 collective-permute-start.4
  37.5 0.4 collective-permute-start.5
  37.9 1.3 %collective-permute-done.6.refs_1_ = bf16[144,2304]{1,0:T(8,128)(2,1)S(1)} collective-permute-done((bf16[144,2304]{1,0:T(8,128)(2,1)S(1)}, bf16[144,2304]{1,0:T(8,128)(2,1)S(1)}, u32[]{:S(2)}, u32[]{:S(2)}) %collective-permute-start.6) | collective-permute-done | bytes 663584 | tf_op jit(solution)/shard_map/ppermute | solution.py:599
  39.2 2.0 %weight_terms.1 = bf16[16,48,768]{2,1,0:T(8,128)(2,1)} custom-call(bf16[144,2304]{1,0:T(8,128)(2,1)S(1)} %get-tuple-element.38.refs_0_, bf16[144,2304]{1,0:T(8,128)(2,1)S(1)} %collective-permute-done.6.refs_1_), custom_call_target="tpu_custom_call" | custom-call | flops 3000000000 | bytes 4000000 | tf_op jit(solution)/shard_map/weight_terms/pallas_call | solution.py:555
  41.2 6.3 %collective-permute-done.3.refs_0_ = bf16[36,1536]{1,0:T(8,128)(2,1)S(1)} collective-permute-done((bf16[36,1536]{1,0:T(8,128)(2,1)S(1)}, bf16[36,1536]{1,0:T(8,128)(2,1)S(1)}, u32[]{:S(2)}, u32[]{:S(2)}) %collective-permute-start.3) | collective-permute-done | bytes 110624 | tf_op jit(solution)/shard_map/ppermute | solution.py:580
  47.6 3.7 %all-to-all-start = ((bf16[16,48,768]{2,1,0:T(8,128)(2,1)}), bf16[16,48,768]{2,1,0:T(8,128)(2,1)S(1)}, u32[]{:S(2)}, u32[]{:S(2)}) async-start(bf16[16,48,768]{2,1,0:T(8,128)(2,1)} %weight_terms.1), calls=%async_computation | async-start | bytes 2359296 | tf_op jit(solution)/shard_map/all_to_all | solution.py:610
  51.3 9.6 %first_backward.1 = (bf16[72,2,768]{2,1,0:T(2,128)(2,1)}, bf16[72,2,768]{2,1,0:T(2,128)(2,1)}) custom-call(bf16[36,1536]{1,0:T(8,128)(2,1)} %copy-done.11, bf16[36,1536]{1,0:T(8,128)(2,1)} %copy-done.12, bf16[36,1536]{1,0:T(8,128)(2,1)} %copy-done.13, bf16[36,1536]{1,0:T(8,128)(2,1)} %copy-done.10, bf16[144,768]{1,0:T(8,128)(2,1)} %get-tuple-element.33.refs_4_, ...), custom_call_target="tpu_custom_call" | custom-call | flops 8999999488 | bytes 4000000 | tf_op jit(solution)/shard_map/first_backward/pallas_call | solution.py:555
  60.9 9.3 %all-to-all-done.refs_0_ = bf16[16,48,768]{2,1,0:T(8,128)(2,1)S(1)} async-done(((bf16[16,48,768]{2,1,0:T(8,128)(2,1)}), bf16[16,48,768]{2,1,0:T(8,128)(2,1)S(1)}, u32[]{:S(2)}, u32[]{:S(2)}) %all-to-all-start) | async-done | bytes 1179680 | tf_op jit(solution)/shard_map/all_to_all | solution.py:610
  70.2 0.9 %copy-done.2 = bf16[72,2,768]{2,1,0:T(2,128)(2,1)S(1)} copy-done((bf16[72,2,768]{2,1,0:T(2,128)(2,1)S(1)}, bf16[72,2,768]{2,1,0:T(2,128)(2,1)}, u32[]{:S(2)}) %copy-start.2) | copy-done | bytes 221208
  71.2 0.3 sum_plane.1
  71.4 14.2 %all_to_all.10.refs_0_ = bf16[16,36,128]{2,1,0:T(8,128)(2,1)S(1)} all-to-all(bf16[16,36,128]{2,1,0:T(8,128)(2,1)S(1)} %sum_plane.1), channel_id=1, replica_groups=mesh['member'=2,'lat'=8,'pair'=8,'core'=2] {'member','lat'}, dimensions={0} | all-to-all | bytes 294912 | tf_op jit(solution)/shard_map/all_to_all | solution.py:620
  85.7 0.7 sum_lat.1
  (28 shorter events, 0.1 us)
Async XLA Ops:
  0.6 20.5 %copy-start.3 = (f32[2,1,759,24]{2,3,1,0:T(8,128)S(1)}, f32[2,1,759,24]{2,3,1,0:T(8,128)}, u32[]{:S(2)}) copy-start(f32[2,1,759,24]{2,3,1,0:T(8,128)} %param.18) | copy-start | bytes 437188
  0.6 20.5 %copy-start.7 = (s32[2,6,12]{2,0,1:T(2,128)S(1)}, s32[2,6,12]{2,0,1:T(2,128)}, u32[]{:S(2)}) copy-start(s32[2,6,12]{2,0,1:T(2,128)} %param.20) | copy-start | bytes 1732
  0.7 20.5 %copy-start.8 = (bf16[144,12]{1,0:T(8,128)(2,1)S(1)}, bf16[144,12]{1,0:T(8,128)(2,1)}, u32[]{:S(2)}) copy-start(bf16[144,12]{1,0:T(8,128)(2,1)} %constant.26.clone.refs_3_) | copy-start | bytes 10372
  0.7 20.5 %copy-start.9 = (bf16[144,12]{1,0:T(8,128)(2,1)S(1)}, bf16[144,12]{1,0:T(8,128)(2,1)}, u32[]{:S(2)}) copy-start(bf16[144,12]{1,0:T(8,128)(2,1)} %constant.25.clone.refs_2_) | copy-start | bytes 10372
  10.4 17.2 %collective-permute-start = (bf16[36,2304]{1,0:T(8,128)(2,1)}, bf16[36,2304]{1,0:T(8,128)(2,1)S(1)}, u32[]{:S(2)}, u32[]{:S(2)}) collective-permute-start(bf16[36,2304]{1,0:T(8,128)(2,1)} %get-tuple-element.23), channel_id=1, source_target_pairs={{0,15},{1,0},{2,1},{3,2},{4,3},{5,4},{6,5},{7,6},{8,7},{9,8},{10,9... | collective-permute-start | bytes 497672 | tf_op jit(solution)/shard_map/ppermute | solution.py:580
  15.3 12.3 %collective-permute-start.1 = (bf16[36,2304]{1,0:T(8,128)(2,1)}, bf16[36,2304]{1,0:T(8,128)(2,1)S(1)}, u32[]{:S(2)}, u32[]{:S(2)}) collective-permute-start(bf16[36,2304]{1,0:T(8,128)(2,1)} %get-tuple-element.24), channel_id=1, source_target_pairs={{0,112},{1,113},{2,114},{3,115},{4,116},{5,117},{6,118},{7,119},{8... | collective-permute-start | bytes 497672 | tf_op jit(solution)/shard_map/ppermute | solution.py:580
  15.4 12.2 %collective-permute-start.2 = (bf16[36,2304]{1,0:T(8,128)(2,1)}, bf16[36,2304]{1,0:T(8,128)(2,1)S(1)}, u32[]{:S(2)}, u32[]{:S(2)}) collective-permute-start(bf16[36,2304]{1,0:T(8,128)(2,1)} %get-tuple-element.25), channel_id=1, source_target_pairs={{0,127},{1,112},{2,113},{3,114},{4,115},{5,116},{6,117},{7,118},{8... | collective-permute-start | bytes 497672 | tf_op jit(solution)/shard_map/ppermute | solution.py:580
  21.1 0.9 %copy-start.6 = (s32[144,256]{1,0:T(8,128)S(1)}, s32[144,256]{1,0:T(8,128)}, u32[]{:S(2)}) copy-start(s32[144,256]{1,0:T(8,128)} %get-tuple-element.26.refs_5_) | copy-start | bytes 442372
  22.0 5.6 %copy-start = (bf16[2,768,2304]{2,1,0:T(8,128)(2,1)S(1)}, bf16[2,768,2304]{2,1,0:T(8,128)(2,1)}, u32[]{:S(2)}) copy-start(bf16[2,768,2304]{2,1,0:T(8,128)(2,1)} %refs_12_.1) | copy-start | bytes 21233668
  22.0 5.6 %copy-start.1 = (bf16[2,768,768]{2,1,0:T(8,128)(2,1)S(1)}, bf16[2,768,768]{2,1,0:T(8,128)(2,1)}, u32[]{:S(2)}) copy-start(bf16[2,768,768]{2,1,0:T(8,128)(2,1)} %refs_7_.3) | copy-start | bytes 7077892
  22.0 5.6 %copy-start.4 = (f32[2,768]{1,0:T(2,128)S(1)}, f32[2,768]{1,0:T(2,128)}, u32[]{:S(2)}) copy-start(f32[2,768]{1,0:T(2,128)} %refs_8_.3) | copy-start | bytes 18436
  22.0 5.6 %copy-start.5 = (bf16[36,2304]{1,0:T(8,128)(2,1)S(1)}, bf16[36,2304]{1,0:T(8,128)(2,1)}, u32[]{:S(2)}) copy-start(bf16[36,2304]{1,0:T(8,128)(2,1)} %get-tuple-element.22.refs_0_) | copy-start | bytes 497668
  37.0 4.2 %copy-start.10 = (bf16[36,1536]{1,0:T(8,128)(2,1)}, bf16[36,1536]{1,0:T(8,128)(2,1)S(1)}, u32[]{:S(2)}) copy-start(bf16[36,1536]{1,0:T(8,128)(2,1)S(1)} %get-tuple-element.32.refs_3_) | copy-start | bytes 331780
  37.0 2.2 %collective-permute-start.6 = (bf16[144,2304]{1,0:T(8,128)(2,1)S(1)}, bf16[144,2304]{1,0:T(8,128)(2,1)S(1)}, u32[]{:S(2)}, u32[]{:S(2)}) collective-permute-start(bf16[144,2304]{1,0:T(8,128)(2,1)S(1)} %get-tuple-element.39), channel_id=1, source_target_pairs={{0,1},{1,0},{2,3},{3,2},{4,5},{5,4},{6,7},{7,6},{8,9},{9,8},{10,11... | collective-permute-start | bytes 1990664 | tf_op jit(solution)/shard_map/ppermute | solution.py:599
  37.4 10.2 %collective-permute-start.3 = (bf16[36,1536]{1,0:T(8,128)(2,1)S(1)}, bf16[36,1536]{1,0:T(8,128)(2,1)S(1)}, u32[]{:S(2)}, u32[]{:S(2)}) collective-permute-start(bf16[36,1536]{1,0:T(8,128)(2,1)S(1)} %get-tuple-element.29), channel_id=1, source_target_pairs={{0,17},{1,18},{2,19},{3,20},{4,21},{5,22},{6,23},{7,24},{8,25},{9,... | collective-permute-start | bytes 331784 | tf_op jit(solution)/shard_map/ppermute | solution.py:580
  37.4 10.1 %collective-permute-start.4 = (bf16[36,1536]{1,0:T(8,128)(2,1)S(1)}, bf16[36,1536]{1,0:T(8,128)(2,1)S(1)}, u32[]{:S(2)}, u32[]{:S(2)}) collective-permute-start(bf16[36,1536]{1,0:T(8,128)(2,1)S(1)} %get-tuple-element.30), channel_id=1, source_target_pairs={{0,16},{1,17},{2,18},{3,19},{4,20},{5,21},{6,22},{7,23},{8,24},{9,... | collective-permute-start | bytes 331784 | tf_op jit(solution)/shard_map/ppermute | solution.py:580
  37.5 10.1 %collective-permute-start.5 = (bf16[36,1536]{1,0:T(8,128)(2,1)S(1)}, bf16[36,1536]{1,0:T(8,128)(2,1)S(1)}, u32[]{:S(2)}, u32[]{:S(2)}) collective-permute-start(bf16[36,1536]{1,0:T(8,128)(2,1)S(1)} %get-tuple-element.31), channel_id=1, source_target_pairs={{0,1},{1,2},{2,3},{3,4},{4,5},{5,6},{6,7},{7,8},{8,9},{9,10},{10,1... | collective-permute-start | bytes 331784 | tf_op jit(solution)/shard_map/ppermute | solution.py:580
  47.6 3.7 %copy-start.11 = (bf16[36,1536]{1,0:T(8,128)(2,1)}, bf16[36,1536]{1,0:T(8,128)(2,1)S(1)}, u32[]{:S(2)}) copy-start(bf16[36,1536]{1,0:T(8,128)(2,1)S(1)} %collective-permute-done.3.refs_0_) | copy-start | bytes 331780
  47.6 3.7 %copy-start.12 = (bf16[36,1536]{1,0:T(8,128)(2,1)}, bf16[36,1536]{1,0:T(8,128)(2,1)S(1)}, u32[]{:S(2)}) copy-start(bf16[36,1536]{1,0:T(8,128)(2,1)S(1)} %collective-permute-done.4.refs_1_) | copy-start | bytes 331780
  47.6 3.8 %copy-start.13 = (bf16[36,1536]{1,0:T(8,128)(2,1)}, bf16[36,1536]{1,0:T(8,128)(2,1)S(1)}, u32[]{:S(2)}) copy-start(bf16[36,1536]{1,0:T(8,128)(2,1)S(1)} %collective-permute-done.5.refs_2_) | copy-start | bytes 331780
  47.6 22.6 %all-to-all-start = ((bf16[16,48,768]{2,1,0:T(8,128)(2,1)}), bf16[16,48,768]{2,1,0:T(8,128)(2,1)S(1)}, u32[]{:S(2)}, u32[]{:S(2)}) async-start(bf16[16,48,768]{2,1,0:T(8,128)(2,1)} %weight_terms.1), calls=%async_computation | async-start | bytes 2359296 | tf_op jit(solution)/shard_map/all_to_all | solution.py:610
  70.2 0.9 %copy-start.2 = (bf16[72,2,768]{2,1,0:T(2,128)(2,1)S(1)}, bf16[72,2,768]{2,1,0:T(2,128)(2,1)}, u32[]{:S(2)}) copy-start(bf16[72,2,768]{2,1,0:T(2,128)(2,1)} %get-tuple-element.37.refs_1_) | copy-start | bytes 663556
